TPU v7x, 32 devices: a whole 2x2x4 slice. The times are simulated.
32 devices in a mesh: dp: 8 (over z, y), narrow: 4 (over x, core).
Axes of the slice: x: 2, y: 2, z: 4, core: 2. Of those that a mesh axis runs over, the one named last changes fastest.
Arguments:
- tokens: bfloat16 [25088, 768], P(('dp', 'narrow')), may hold values from -6 to 6
- input_projection: bfloat16 [3, 768, 768], P(None, None, 'narrow'), may hold values from -0.21875 to 0.21875
- input_bias: float32 [2, 768], replicated, may hold values from -3 to 3
- position_bias: float32 [169, 24], replicated, may hold values from -4 to 4
- output_projection: bfloat16 [768, 768], P('narrow'), may hold values from -0.5 to 0.5
- inner_weight: bfloat16 [768, 3072], P(None, 'narrow'), may hold values from -0.21875 to 0.21875
- inner_bias: float32 [3072], replicated, may hold values from -2 to 2
- outer_weight: bfloat16 [3072, 768], P('narrow'), may hold values from -0.109375 to 0.109375
- norm_gains: float32 [3, 768], replicated, may hold values from 0.5 to 1.5
- offsets: float32 [5, 768], replicated, may hold values from -2 to 2
- head_first: bfloat16 [768, 2048], replicated, may hold values from -0.21875 to 0.21875
- head_first_bias: float32 [2048], replicated, may hold values from -2 to 2
- head_second: bfloat16 [2048, 2048], replicated, may hold values from -0.125 to 0.125
- head_second_bias: float32 [2048], replicated, may hold values from -2 to 2
- head_third: bfloat16 [2048, 256], replicated, may hold values from -0.125 to 0.125
- head_third_bias: float32 [256], replicated, may hold values from -2 to 2
- prototype_direction: bfloat16 [256, 65536], P(None, ('dp', 'narrow')), may hold values from -6 to 6
- prototype_gain: float32 [65536], P(('dp', 'narrow')), may hold values from 10 to 40
- crop_windows: int32 [8, 4], P('dp'), may hold values from 1 to 49, as said below
- first_epoch: int32 [65536], P(('dp', 'narrow')), may hold values 0 or 1
- feature_cotangent: bfloat16 [25088, 768], P(('dp', 'narrow')), may hold values from -6 to 6
- logit_cotangent: bfloat16 [32, 65536], P(None, ('dp', 'narrow')), may hold values from -6 to 6
Outputs:
- features: bfloat16 [25088, 768], P(('dp', 'narrow'))
- logits: float32 [32, 65536], P(None, ('dp', 'narrow'))
- tokens_grad: float32 [25088, 768], P(('dp', 'narrow'))
- input_projection_grad: float32 [3, 768, 768], P(None, 'dp', 'narrow')
- input_bias_grad: float32 [2, 768], replicated
- position_bias_grad: float32 [169, 24], replicated
- output_projection_grad: float32 [768, 768], P('narrow', 'dp')
- inner_weight_grad: float32 [768, 3072], P('dp', 'narrow')
- inner_bias_grad: float32 [3072], replicated
- outer_weight_grad: float32 [3072, 768], P('narrow', 'dp')
- norm_gains_grad: float32 [3, 768], replicated
- offsets_grad: float32 [5, 768], replicated
- head_first_grad: float32 [768, 2048], P(None, 'dp')
- head_first_bias_grad: float32 [2048], P('dp')
- head_second_grad: float32 [2048, 2048], P(None, 'dp')
- head_second_bias_grad: float32 [2048], P('dp')
- head_third_grad: float32 [2048, 256], P('dp')
- head_third_bias_grad: float32 [256], P('dp')
- prototype_direction_grad: float32 [256, 65536], P(None, ('dp', 'narrow'))
- prototype_gain_grad: float32 [65536], P(('dp', 'narrow'))
Inputs may be any that keep to these rules, and one draw needn't show every extreme that they name: `crop_windows`: each row sums to 64; one entry of each row, at a place drawn from the seed, is exactly 49, and the others sum to 15.
All inputs are finite; a program needn't handle non-finite values. No bound on the sum of `first_epoch` on one device may be relied on, other than what follows from the above.
Results may differ from a plain program's by a relative error of at most 0.017.
The roundings to bfloat16 on the way count: a program that leaves them out, or rounds other values in their place, can miss the bound.
Values may be sent and summed in bfloat16 or wider, within the bound.
No kernel may reach another device: no remote copies, remote signals or barrier semaphores. Data moves between devices by JAX's collectives and lax.ppermute only.
A program may use at most 192 MiB of HBM per device.

v0:
```python
import functools

import jax
import jax.numpy as jnp
from jax import lax
from jax.experimental import pallas as pl
from jax.experimental.pallas import tpu as pltpu
from jax.sharding import PartitionSpec as P

HIGH = lax.Precision.HIGHEST
F32 = jnp.float32
BF16 = jnp.bfloat16
SIDE = 7
SPOTS = SIDE * SIDE
PAD = 64
LANES = 128
CHUNK = 112
VMEM_LIMIT = 60 * 1024 * 1024
NEG = -1e30


def dot(left, right):
    return jnp.dot(left, right, preferred_element_type=F32)


def dot_left(left, right):
    return lax.dot_general(left, right, (((0,), (0,)), ((), ())), preferred_element_type=F32)


def dot_right(left, right):
    return lax.dot_general(left, right, (((1,), (1,)), ((), ())), preferred_element_type=F32)


def cost(us):
    return pl.CostEstimate(flops=0, bytes_accessed=int(us * 3.3e6), transcendentals=0)


def call(body, outs, ins, **kw):
    scratch = kw.pop("scratch", ())
    return pl.pallas_call(
        body,
        out_shape=outs,
        in_specs=[pl.BlockSpec(memory_space=pltpu.VMEM)] * len(ins),
        out_specs=jax.tree.map(lambda _: pl.BlockSpec(memory_space=pltpu.VMEM), outs),
        scratch_shapes=scratch,
        compiler_params=pltpu.CompilerParams(vmem_limit_bytes=VMEM_LIMIT),
        cost_estimate=cost(kw.pop("us")),
        **kw,
    )(*ins)


def shape(dims, kind):
    return jax.ShapeDtypeStruct(dims, kind)


def norm_parts(values):
    center = values - jnp.mean(values, axis=-1, keepdims=True)
    spread = jnp.mean(center * center, axis=-1, keepdims=True)
    inv = lax.rsqrt(spread + 1e-05)
    return center * inv, inv


def norm_back(nhat, inv, gain, grad):
    scaled = grad * gain
    first = jnp.mean(scaled, axis=-1, keepdims=True)
    second = jnp.mean(scaled * nhat, axis=-1, keepdims=True)
    return (scaled - first - nhat * second) * inv


def gelu_pair(pre):
    bell = jnp.exp(pre * pre * -0.5)
    dist = jnp.abs(pre) * (0.3275911 * 0.70710678118654752) + 1.0
    inv = 1.0 / dist
    poly = 0.5 * 1.061405429
    for coef in (-1.453152027, 1.421413741, -0.284496736, 0.254829592):
        poly = poly * inv + 0.5 * coef
    tail = poly * inv * bell
    cdf = jnp.where(pre < 0.0, tail, 1.0 - tail)
    return pre * cdf, cdf + pre * (bell * 0.3989422804014327)


def widen(windows, flat, padded):
    place = lax.broadcasted_iota(jnp.int32, (PAD, 1), 0)
    for w in range(windows):
        block = flat[w * SPOTS : w * SPOTS + PAD, :]
        padded[w * PAD : (w + 1) * PAD, :] = jnp.where(place < SPOTS, block, 0.0).astype(BF16)


def norm_one_body(windows, tokens, gains, offsets, padded, flat):
    for r in range(0, tokens.shape[0], CHUNK):
        nhat, _ = norm_parts(tokens[r : r + CHUNK, :].astype(F32))
        flat[r : r + CHUNK, :] = nhat * gains[0:1, :] + offsets[0:1, :]
    widen(windows, flat, padded)


def head_masks(size):
    lane = lax.broadcasted_iota(jnp.int32, (PAD, LANES), 1) // size
    return [lane == h for h in range(LANES // size)]


def spread_heads(values, masks):
    zero = jnp.zeros_like(values)
    return jnp.concatenate([jnp.where(m, values, zero) for m in masks], axis=0)


def fold_heads(values, masks):
    total = values[0:PAD, :]
    for h in range(1, len(masks)):
        total = jnp.where(masks[h], values[h * PAD : (h + 1) * PAD, :], total)
    return total


def attend_body(size, scale, padded, near, far, bias, table, qkv_out, p_out, att_out, stacked):
    quarter = near.shape[1]
    width = 2 * quarter
    per = LANES // size * PAD

    @pl.when(pl.program_id(0) == 0)
    def _():
        stacked[:, 0:quarter, :] = near[...]
        stacked[:, quarter:width, :] = far[...]

    x = padded[...]
    q = (dot_right(x, stacked[0]) + bias[0:1, :]).astype(BF16)
    k = dot_right(x, stacked[1]).astype(BF16)
    v = (dot_right(x, stacked[2]) + bias[1:2, :]).astype(BF16)
    qkv_out[:, 0:width] = q
    qkv_out[:, width : 2 * width] = k
    qkv_out[:, 2 * width : 3 * width] = v
    masks = head_masks(size)
    items = [
        (slice(w * PAD, (w + 1) * PAD), g) for w in range(x.shape[0] // PAD) for g in range(width // LANES)
    ]
    lanes = lambda g: slice(g * LANES, (g + 1) * LANES)
    scores = [
        dot_right(k[r, lanes(g)], spread_heads(q[r, lanes(g)], masks)) * scale
        + table[:, g * per : (g + 1) * per]
        for r, g in items
    ]
    e = [jnp.exp(s - jnp.max(s, axis=0, keepdims=True)) for s in scores]
    probs = [(s * (1.0 / jnp.sum(s, axis=0, keepdims=True))).astype(BF16) for s in e]
    folded = [fold_heads(dot_left(p, v[r, lanes(g)]), masks) for p, (r, g) in zip(probs, items)]
    for (r, g), p, o in zip(items, probs, folded):
        p_out[r, g * per : (g + 1) * per] = p
        att_out[r, lanes(g)] = o.astype(BF16)


def attend_back_body(size, scale, low, weight, qkv0, qkv1, p0, p1, d_out, table_out, sums_out):
    width = qkv0.shape[1] // 3
    per = LANES // size * PAD
    pair_groups = width // LANES

    @pl.when(pl.program_id(0) == 0)
    def _():
        table_out[...] = jnp.zeros_like(table_out)
        sums_out[...] = jnp.zeros_like(sums_out)

    given = dot_right(low[...], weight[...]).astype(BF16)
    masks = head_masks(size)
    windows = low.shape[0] // PAD
    both = 2
    for first in range(0, windows, both):
        items = [
            (slice(w * PAD, (w + 1) * PAD), pair, g)
            for w in range(first, first + both)
            for pair in range(2)
            for g in range(pair_groups)
        ]
        qkv = (qkv0, qkv1)
        probs_of = (p0, p1)

        def part(item, t):
            r, pair, g = item
            return qkv[pair][r, t * width + g * LANES : t * width + (g + 1) * LANES]

        gs = [
            spread_heads(given[r, pair * width + g * LANES : pair * width + (g + 1) * LANES], masks)
            for r, pair, g in items
        ]
        prob_grad = [dot_right(part(i, 2), s) for i, s in zip(items, gs)]
        low_probs = [probs_of[pair][r, g * per : (g + 1) * per] for r, pair, g in items]
        probs = [p.astype(F32) for p in low_probs]
        weighed = [p * s for p, s in zip(probs, prob_grad)]
        score_low = [
            (t - p * jnp.sum(t, axis=0, keepdims=True)).astype(BF16) for p, t in zip(probs, weighed)
        ]
        dv = [dot(p, s).astype(BF16) for p, s in zip(low_probs, gs)]
        dk = [
            (dot(s, spread_heads(part(i, 0), masks)) * scale).astype(BF16)
            for i, s in zip(items, score_low)
        ]
        dq = [
            (fold_heads(dot_left(s, part(i, 1)), masks) * scale).astype(BF16)
            for i, s in zip(items, score_low)
        ]
        for (r, pair, g), *parts in zip(items, dq, dk, dv):
            for t, value in enumerate(parts):
                at = (pair * 3 + t) * width + g * LANES
                d_out[r, at : at + LANES] = value
        for pair in range(2):
            for g in range(pair_groups):
                mine = [n for n, (_, p, h) in enumerate(items) if (p, h) == (pair, g)]
                at = (pair * pair_groups + g) * per
                table_out[:, at : at + per] += sum(score_low[n].astype(F32) for n in mine)
                for t, values in enumerate((dq, dk, dv)):
                    at = (pair * 3 + t) * width + g * LANES
                    sums_out[0:1, at : at + LANES] += sum(
                        jnp.sum(values[n].astype(F32), axis=0, keepdims=True) for n in mine
                    )


def mixed_body(windows, count, att0, att1, *refs):
    wo = refs[:count]
    tokens, gains, offsets, mixed, normed, stacked = refs[count:]
    quarter = wo[0].shape[0]
    half = att0.shape[1]
    for k in range(count):
        stacked[k * quarter : (k + 1) * quarter, :] = wo[k][...]
    group = 4
    for first in range(0, windows, group):
        here = slice(first * PAD, (first + group) * PAD)
        total = dot(att0[here, :], stacked[0:half, :]) + dot(att1[here, :], stacked[half : 2 * half, :])
        for w in range(group):
            at = (first + w) * SPOTS
            mixed[at : at + SPOTS, :] = total[w * PAD : w * PAD + SPOTS, :]
    for r in range(0, tokens.shape[0], CHUNK):
        rows = slice(r, r + CHUNK)
        value = tokens[rows, :].astype(F32) + mixed[rows, :] + offsets[1:2, :]
        mixed[rows, :] = value
        nhat, _ = norm_parts(value)
        normed[rows, :] = (nhat * gains[1:2, :] + offsets[2:3, :]).astype(BF16)


def copies_of(pairs, sems, first=0):
    return [pltpu.make_async_copy(a, b, sems.at[first + i]) for i, (a, b) in enumerate(pairs)]


def pieces_of(pieces, target):
    at, pairs = 0, []
    for p in pieces:
        pairs.append((p, target.at[pl.ds(at, p.shape[0]), :]))
        at += p.shape[0]
    return pairs


def inner_body(count, pieces, started, last, *refs):
    refs = list(refs)
    take = lambda n: [refs.pop(0) for _ in range(n)]
    normed, bias = take(2)
    wi = take(count)
    wo = [take(pieces) for _ in range(count)]
    before = take(1)[0] if started else None
    if last:
        mixed, gains, offsets, crop = take(4)
    act_out, slope_out = take(count), take(count)
    if last:
        block_out, features, pool = take(3)
    else:
        total_out = take(1)[0]
    x, wi_v, wo_v, act, slope, total, sems, out_sems = take(8)
    if last:
        mixed_v = take(1)[0]
    pairs = [(normed, x)]
    for k in range(count):
        pairs += [(wi[k], wi_v.at[k])] + pieces_of(wo[k], wo_v.at[k])
    if started:
        pairs.append((before, total))
    if last:
        pairs.append((mixed, mixed_v))
    copies = copies_of(pairs, sems)
    for c in copies:
        c.start()
    copies.pop(0).wait()
    weights = [[copies.pop(0) for _ in range(1 + pieces)] for _ in range(count)]
    half = x.shape[0] // 2
    work = [(k, h) for k in range(count) for h in range(2)]

    def first(k, h):
        if h == 0:
            weights[k][0].wait()
        return dot(x[h * half : (h + 1) * half, :], wi_v[k]) + bias[k]

    out_pairs = [p for k in range(count) for p in ((act.at[k], act_out[k]), (slope.at[k], slope_out[k]))]
    if not last:
        out_pairs.append((total, total_out))
    outs = copies_of(out_pairs, out_sems)
    ahead = first(*work[0])
    for n, (k, h) in enumerate(work):
        pre = ahead
        if n + 1 < len(work):
            ahead = first(*work[n + 1])
        rows = slice(h * half, (h + 1) * half)
        value, grad = gelu_pair(pre)
        value = value.astype(BF16)
        act[k, rows, :] = value
        slope[k, rows, :] = grad.astype(BF16)
        if h == 1:
            outs[2 * k].start()
            outs[2 * k + 1].start()
        else:
            for c in weights[k][1:]:
                c.wait()
            if n == 0 and started:
                copies.pop(0).wait()
        share = dot(value, wo_v[k])
        if k == 0 and not started:
            total[rows, :] = share
        else:
            total[rows, :] += share
    if last:
        copies.pop(0).wait()
        crops = pool.shape[0]
        sums = [jnp.zeros((1, total.shape[1]), F32)] * crops
        for r in range(0, total.shape[0], CHUNK):
            rows = slice(r, r + CHUNK)
            value = mixed_v[rows, :] + total[rows, :] + offsets[3:4, :]
            block_out[rows, :] = value
            features[rows, :] = value.astype(BF16)
            nhat, _ = norm_parts(value)
            head = nhat * gains[2:3, :] + offsets[4:5, :]
            for c in range(crops):
                sums[c] = sums[c] + jnp.sum(jnp.where(crop[rows, :] == c, head, 0.0), axis=0, keepdims=True)
        for c in range(crops):
            pool[c : c + 1, :] = sums[c]
    else:
        outs[-1].start()
    for c in outs:
        c.wait()


def head_back_body(block_out, cotangent, crop, pooled_grad, gains, grad_out, low_out, sums_out):
    crops = pooled_grad.shape[0]

    @pl.when(pl.program_id(0) == 0)
    def _():
        sums_out[...] = jnp.zeros_like(sums_out)

    nhat, inv = norm_parts(block_out[...])
    grad = jnp.zeros(nhat.shape, F32)
    for c in range(crops):
        grad = jnp.where(crop[...] == c, pooled_grad[c : c + 1, :], grad)
    out = cotangent[...].astype(F32) + norm_back(nhat, inv, gains[2:3, :], grad)
    grad_out[...] = out
    low_out[...] = out.astype(BF16)
    sums_out[0:1, :] += jnp.sum(grad * nhat, axis=0, keepdims=True)
    sums_out[1:2, :] += jnp.sum(grad, axis=0, keepdims=True)
    sums_out[2:3, :] += jnp.sum(out, axis=0, keepdims=True)


def head_body(
    pooled, unit_grad, first_hbm, second_hbm, third_hbm, first_bias, second_bias, third_bias,
    first_act, second_act, units, embed_grad, second_low, first_low, pooled_grad,
    first, second, third, sems,
):
    chunk = 512
    parts = second.shape[0] // chunk
    rows_of = lambda i: pl.ds(i * chunk, chunk)
    pairs = [(first_hbm, first)]
    pairs += [(second_hbm.at[rows_of(i), :], second.at[rows_of(i), :]) for i in range(parts)]
    pairs += [(third_hbm, third)]
    copies = copies_of(pairs, sems)
    for c in copies:
        c.start()
    copies[0].wait()
    act, first_slope = gelu_pair(dot(pooled[...], first[...]) + first_bias[...])
    act = act.astype(BF16)
    first_act[...] = act
    total = second_bias[...]
    for i in range(parts):
        copies[1 + i].wait()
        total = total + dot(act[:, i * chunk : (i + 1) * chunk], second[i * chunk : (i + 1) * chunk, :])
    act, second_slope = gelu_pair(total)
    act = act.astype(BF16)
    second_act[...] = act
    copies[-1].wait()
    embedded = dot(act, third[...]) + third_bias[...]
    inv = lax.rsqrt(jnp.sum(embedded * embedded, axis=-1, keepdims=True) + 1e-06)
    units[...] = (embedded * inv).astype(BF16)
    given = unit_grad[...]
    along = jnp.sum(embedded * given, axis=-1, keepdims=True)
    grad = inv * given - (inv * inv * inv) * embedded * along
    embed_grad[...] = grad
    low = (dot_right(grad.astype(BF16), third[...]) * second_slope).astype(BF16)
    second_low[...] = low
    low = (dot_right(low, second[...]) * first_slope).astype(BF16)
    first_low[...] = low
    pooled_grad[...] = dot_right(low, first[...])


def inner_back_body(windows, pieces, started, last, *refs):
    refs = list(refs)
    take = lambda n: [refs.pop(0) for _ in range(n)]
    count = len(pieces)
    low_in, normed = take(2)
    act_in, slope_in, wi_in = take(count), take(count), take(count)
    wo_in = [take(n) for n in pieces]
    before = take(1)[0] if started else None
    if last:
        mixed, out_grad, gains = take(3)
    outer_out, inner_out = take(count), take(count)
    sums_out = take(1)[0]
    if last:
        grad_out, low_out, norm_sums = take(3)
    else:
        total_out = take(1)[0]
    low, x, act, slope, wi, wo, outer, inner, pre, total, sems, out_sems = take(12)
    first_of = []
    pairs = [(low_in, low)]
    for k in range(count):
        first_of.append(len(pairs))
        pairs += pieces_of(wo_in[k], wo.at[k]) + [(slope_in[k], slope.at[k]), (act_in[k], act.at[k])]
        pairs += [(normed, x)] * (k == 0) + [(wi_in[k], wi.at[k])]
    if started:
        pairs.append((before, total))
    rows_all = total.shape[0]
    if last:
        mixed_v, flat = take(2)
        pairs += [(mixed, mixed_v), (out_grad, flat.at[pl.ds(0, rows_all), :])]
    copies = copies_of(pairs, sems)
    for c in copies:
        c.start()
    wait = lambda n: [copies.pop(0).wait() for _ in range(n)]
    out_pairs = [p for k in range(count) for p in ((outer.at[k], outer_out[k]), (inner.at[k], inner_out[k]))]
    outs = copies_of(out_pairs + ([] if last else [(total, total_out)]), out_sems)
    wait(1)
    for k in range(count):
        wait(pieces[k])
        raw = dot_right(low[...], wo[k])
        wait(2)
        outer_value = dot_left(low[...], act[k])
        value = (raw * slope[k].astype(F32)).astype(BF16)
        pre[k] = value
        sums_out[k : k + 1, :] = jnp.sum(value.astype(F32), axis=0, keepdims=True)
        outer[k] = outer_value.astype(BF16)
        outs[2 * k].start()
        wait(2 if k == 0 else 1)
        inner[k] = dot_left(x[...], pre[k]).astype(BF16)
        outs[2 * k + 1].start()
        share = dot_right(pre[k], wi[k])
        if k == 0 and not started:
            total[...] = share
        else:
            if k == 0:
                copies.pop(sum(pieces[1:]) + 3 * (count - 1)).wait()
            total[...] += share
    if not last:
        outs[-1].start()
    if last:
        wait(2)
        gain_sum = jnp.zeros((1, total.shape[1]), F32)
        shift_sum = gain_sum
        bias_sum = gain_sum
        for r in range(0, rows_all, CHUNK):
            rows = slice(r, r + CHUNK)
            nhat, inv = norm_parts(mixed_v[rows, :])
            grad = total[rows, :]
            gain_sum = gain_sum + jnp.sum(grad * nhat, axis=0, keepdims=True)
            shift_sum = shift_sum + jnp.sum(grad, axis=0, keepdims=True)
            out = flat[rows, :] + norm_back(nhat, inv, gains[1:2, :], grad)
            bias_sum = bias_sum + jnp.sum(out, axis=0, keepdims=True)
            grad_out[rows, :] = out
            flat[rows, :] = out
        norm_sums[0:1, :] = gain_sum
        norm_sums[1:2, :] = shift_sum
        norm_sums[2:3, :] = bias_sum
        widen(windows, flat, low_out)
    for c in outs:
        c.wait()


def weight_grad_body(x, low, d, att0, att1, even_a, odd_a, even_b, odd_b):
    width = att0.shape[1]
    quarter = width // 2
    big = dot_left(x[...], d[...])
    for t, (even, odd, at) in enumerate(((even_a, odd_a, 0), (even_a, odd_a, 1), (even_b, odd_b, 0))):
        lanes = slice(at * quarter, (at + 1) * quarter)
        even[0, :, lanes] = big[:, t * width : t * width + quarter].astype(BF16)
        odd[0, :, lanes] = big[:, t * width + quarter : (t + 1) * width].astype(BF16)
    for pair, att in enumerate((att0, att1)):

        @pl.when(pl.program_id(0) == 1 - pair)
        def _(att=att):
            side = dot_left(low[...], att[...])
            even_b[0, :, quarter:width] = side[:, 0:quarter].astype(BF16)
            odd_b[0, :, quarter:width] = side[:, quarter:width].astype(BF16)


def tokens_back_body(windows, grads, stacked0, stacked1, tokens, mixed_grad, gains, head, mid, ends, grad_out, packed, flat):
    half = stacked0.shape[0]
    group = 4
    for first in range(0, windows, group):
        here = slice(first * PAD, (first + group) * PAD)
        total = dot(grads[here, 0:half], stacked0[...]) + dot(grads[here, half : 2 * half], stacked1[...])
        for w in range(group):
            at = (first + w) * SPOTS
            flat[at : at + SPOTS, :] = total[w * PAD : w * PAD + SPOTS, :]
    gain_sum = jnp.zeros((1, tokens.shape[1]), F32)
    shift_sum = gain_sum
    for r in range(0, tokens.shape[0], CHUNK):
        rows = slice(r, r + CHUNK)
        nhat, inv = norm_parts(tokens[rows, :].astype(F32))
        grad = flat[rows, :]
        gain_sum = gain_sum + jnp.sum(grad * nhat, axis=0, keepdims=True)
        shift_sum = shift_sum + jnp.sum(grad, axis=0, keepdims=True)
        grad_out[rows, :] = mixed_grad[rows, :] + norm_back(nhat, inv, gains[0:1, :], grad)
    packed[0:1, :] = gain_sum
    packed[1:2, :] = mid[0:1, :]
    packed[2:3, :] = head[0:1, :]
    packed[3:4, :] = shift_sum
    packed[4:5, :] = mid[2:3, :]
    packed[5:6, :] = mid[1:2, :]
    packed[6:7, :] = head[2:3, :]
    packed[7:8, :] = head[1:2, :]
    packed[8 : 8 + ends.shape[0], :] = ends[...]


def swap(values, axis, bit):
    return lax.ppermute(values, axis, [(i, i ^ bit) for i in range(lax.axis_size(axis))])


def bits_of(axis):
    size = lax.axis_size(axis)
    bit, found = 1, []
    while bit < size:
        found.append(bit)
        bit *= 2
    return found


def has_bit(axis, bit):
    return (lax.axis_index(axis) // bit) % 2 == 1


def after(values, *others):
    return lax.optimization_barrier((values, *others))[0]


def sum_over(values, axes):
    for axis in axes:
        for bit in bits_of(axis):
            values = values + swap(values, axis, bit)
    return values


def ordered(mine, other, upper):
    return jnp.concatenate([jnp.where(upper, other, mine), jnp.where(upper, mine, other)], axis=0)


def gather_over(values, axis):
    for bit in bits_of(axis):
        values = ordered(values, swap(values, axis, bit), has_bit(axis, bit))
    return values


def by_distance(values, axis):
    for bit in bits_of(axis):
        size = values.shape[0]
        folded = values.reshape(size // (2 * bit), 2, bit, *values.shape[1:])
        folded = jnp.where(has_bit(axis, bit), folded[:, ::-1], folded)
        values = folded.reshape(values.shape)
    return values


def own_half(values, share, piece=0, pieces=1):
    parts = values.reshape(2 * pieces, values.shape[0] // (2 * pieces), *values.shape[1:])
    return lax.dynamic_index_in_dim(parts, 2 * piece + lax.axis_index("dp") // share % 2, 0, keepdims=False)


def halve_rows(values, bit):
    groups, rows, columns = values.shape
    folded = values.reshape(groups // 2, 2, rows, columns)
    mine = lax.axis_index("dp") // bit % 2
    keep = lax.dynamic_index_in_dim(folded, mine, 1, keepdims=False)
    send = lax.dynamic_index_in_dim(folded, 1 - mine, 1, keepdims=False)
    return keep, send


def add(kept, got):
    return kept.astype(F32) + got.astype(F32)


def offset_table():
    places = jnp.arange(PAD, dtype=jnp.int32)
    row_of = places // SIDE
    col_of = places % SIDE
    offset = (row_of[None, :] - row_of[:, None] + SIDE - 1) * (2 * SIDE - 1) + (
        col_of[None, :] - col_of[:, None] + SIDE - 1
    )
    inside = (places[:, None] < SPOTS) & (places[None, :] < SPOTS)
    offset = jnp.where(inside, offset, -1)
    entries = jnp.arange((2 * SIDE - 1) ** 2, dtype=jnp.int32)
    return (offset.reshape(-1)[:, None] == entries[None, :]).astype(F32)


def shards(
    tokens,
    input_projection,
    input_bias,
    position_bias,
    output_projection,
    inner_weight,
    inner_bias,
    outer_weight,
    norm_gains,
    offsets,
    head_first,
    head_first_bias,
    head_second,
    head_second_bias,
    head_third,
    head_third_bias,
    prototype_direction,
    prototype_gain,
    crop_windows,
    first_epoch,
    feature_cotangent,
    logit_cotangent,
):
    rows, width = tokens.shape
    windows = rows // SPOTS
    narrow_index = lax.axis_index("narrow")
    dp_index = lax.axis_index("dp")
    count = lax.axis_size("narrow")
    groups = lax.axis_size("dp")
    quarter = input_projection.shape[2]
    hidden = inner_weight.shape[1]
    heads = position_bias.shape[1] // count
    size = quarter // heads
    scale = size ** (-0.5)
    crops = crop_windows.shape[1]
    padded_rows = windows * PAD

    near, far = bits_of("narrow")
    data_bits = bits_of("dp")
    share, share_too = data_bits[0], data_bits[1]

    w_in0 = input_projection.swapaxes(1, 2)
    w_in1 = swap(w_in0, "narrow", near)
    in_half = swap(own_half(w_in0.reshape(3 * quarter, width), share), "narrow", far)
    w_att1 = swap(output_projection, "narrow", near)
    w_inner1 = swap(inner_weight, "narrow", near)
    w_outer1 = swap(outer_weight, "narrow", near)

    bias_in = by_distance(input_bias.reshape(2, count, quarter).swapaxes(0, 1), "narrow")
    bias_in = bias_in.swapaxes(0, 1).reshape(2, count * quarter)
    bias_inner = by_distance(inner_bias.reshape(count, 1, hidden), "narrow")
    table = offset_table()
    turned = by_distance(position_bias.T.reshape(count, heads, -1), "narrow").reshape(count * heads, -1)
    spread = jnp.dot(table, turned.T, precision=HIGH, preferred_element_type=F32)
    spread = spread.reshape(PAD, PAD, count * heads).transpose(0, 2, 1)
    inside = (jnp.arange(PAD) < SPOTS)[:, None, None]
    spread = jnp.where(inside, spread, NEG).reshape(PAD, count * heads * PAD)

    ends = jnp.cumsum(crop_windows[0])
    row_window = narrow_index * windows + jnp.arange(rows, dtype=jnp.int32) // SPOTS
    crop_of_row = jnp.sum((row_window[:, None] >= ends[None, :]).astype(jnp.int32), axis=1, keepdims=True)
    crop_tokens = (crop_windows[0] * SPOTS).astype(F32)

    padded = call(
        functools.partial(norm_one_body, windows),
        shape((padded_rows, width), BF16),
        (tokens, norm_gains, offsets),
        scratch=[pltpu.VMEM((rows + 16, width), F32)],
        us=3.5,
    )
    half = 2 * quarter
    pair_lanes = 2 * heads * PAD
    batch = 4 * PAD
    by_row = lambda n: pl.BlockSpec((batch, n), lambda i: (i, 0))
    fixed = lambda *dims: pl.BlockSpec(dims, lambda i: (0,) * len(dims))
    qkv, probs, attended, stacked_in = [], [], [], []

    def attend(pair, x, first, second):
        got = pl.pallas_call(
            functools.partial(attend_body, size, scale),
            grid=(padded_rows // batch,),
            out_shape=(
                shape((padded_rows, 3 * half), BF16),
                shape((padded_rows, pair_lanes), BF16),
                shape((padded_rows, half), BF16),
                shape((3, half, width), BF16),
            ),
            in_specs=[
                by_row(width),
                fixed(3, quarter, width),
                fixed(3, quarter, width),
                fixed(2, half),
                pl.BlockSpec((PAD, pair_lanes), lambda i, pair=pair: (0, pair)),
            ],
            out_specs=(by_row(3 * half), by_row(pair_lanes), by_row(half), fixed(3, half, width)),
            compiler_params=pltpu.CompilerParams(vmem_limit_bytes=VMEM_LIMIT),
            cost_estimate=cost(9.0),
        )(x, first, second, bias_in[:, pair * half : (pair + 1) * half], spread)
        for keep, value in zip((qkv, probs, attended, stacked_in), got):
            keep.append(value)
        return got

    def whole_of(mine, other, bit):
        return ordered(mine, other, has_bit("dp", bit))

    def bring(weight, bit, *others, piece=0, pieces=1):
        return swap(own_half(after(weight, *others), bit, piece, pieces), "narrow", far)

    in_half, w_in1 = after((in_half, w_in1), padded, spread)
    in_rest = swap(in_half, "dp", share)
    w_att2 = swap(after(output_projection, in_half), "narrow", far)
    got = attend(0, after(padded, in_half), w_in0, w_in1)
    in_rest, w_att2 = after((in_rest, w_att2), got)
    inner_half = bring(inner_weight, share, w_att2)
    w_in2 = whole_of(in_half, in_rest, share).reshape(w_in0.shape)
    w_in3 = swap(w_in2, "narrow", near)
    w_att3 = swap(w_att2, "narrow", near)
    got = attend(1, after(padded, got), w_in2, w_in3)
    w_att3, inner_half = after((w_att3, inner_half), got)
    outer_half = bring(outer_weight, share_too, inner_half)
    inner_rest = swap(inner_half, "dp", share)
    mixed, normed_two, stacked_att = call(
        functools.partial(mixed_body, windows, count),
        (shape((rows, width), F32), shape((rows, width), BF16), shape((count * quarter, width), BF16)),
        (
            *attended,
            output_projection, w_att1, w_att2, w_att3,
            after(tokens, inner_half),
            norm_gains,
            offsets,
        ),
        us=6.0,
    )
    anywhere = pl.BlockSpec(memory_space=pl.ANY)
    held = pl.BlockSpec(memory_space=pltpu.VMEM)
    row_held = pltpu.VMEM((rows, width), F32)
    low_held = pltpu.VMEM((rows, width), BF16)
    act_shape = shape((rows, hidden), BF16)

    def inner_call(x, bias, wi, wo, before=(), ending=()):
        n, pieces = len(wi), len(wo[0])
        wo = [p for w in wo for p in w]
        last = bool(ending)
        tail_shape = (shape((rows, width), F32),)
        tail_spec = (anywhere,)
        if last:
            tail_shape += (shape((rows, width), BF16), shape((crops, width), F32))
            tail_spec = (held,) * 3
        return pl.pallas_call(
            functools.partial(inner_body, n, pieces, bool(before), last),
            out_shape=(act_shape,) * (2 * n) + tail_shape,
            in_specs=[anywhere, held] + [anywhere] * (len(wi) + len(wo) + len(before)) + ([anywhere] + [held] * 3 if last else []),
            out_specs=(anywhere,) * (2 * n) + tail_spec,
            scratch_shapes=[
                low_held,
                pltpu.VMEM((n, width, hidden), BF16),
                pltpu.VMEM((n, hidden, width), BF16),
                pltpu.VMEM((n, rows, hidden), BF16),
                pltpu.VMEM((n, rows, hidden), BF16),
                row_held,
                pltpu.SemaphoreType.DMA((1 + n * (1 + pieces) + len(before) + last,)),
                pltpu.SemaphoreType.DMA((2 * n + 1,)),
            ] + ([row_held] if last else []),
            compiler_params=pltpu.CompilerParams(vmem_limit_bytes=VMEM_LIMIT),
            cost_estimate=cost(16.0 if last else 7.0),
        )(x, bias, *wi, *wo, *before, *ending)

    act0, slope0, inner_total = inner_call(normed_two, bias_inner[0:1], [inner_weight], [[outer_weight]])
    outer_half, inner_rest = after((outer_half, inner_rest), inner_total)
    outer_rest = swap(outer_half, "dp", share_too)
    w_inner2 = whole_of(inner_half, inner_rest, share)
    w_inner3 = swap(w_inner2, "narrow", near)
    act1, slope1, inner_total = inner_call(
        after(normed_two, outer_half, w_inner2), bias_inner[1:2], [w_inner1], [[w_outer1]], (inner_total,)
    )
    direction = after(prototype_direction, inner_total).astype(F32)
    column_inv = lax.rsqrt(jnp.sum(direction * direction, axis=0, keepdims=True) + 1e-06)
    columns_low = (prototype_gain * direction * column_inv).astype(BF16)
    unit_share = dot_right(logit_cotangent, columns_low)
    w_inner3, outer_rest = after((w_inner3, outer_rest), unit_share)
    w_outer2 = whole_of(outer_half, outer_rest, share_too)
    w_outer3 = swap(w_outer2, "narrow", near)
    outer2, outer3 = [w_outer2], [w_outer3]
    act2, act3, slope2, slope3, block_out, features, pool = inner_call(
        normed_two, bias_inner[2:4], [w_inner2, w_inner3], [outer2, outer3], (inner_total,),
        (mixed, norm_gains, offsets, crop_of_row),
    )

    flat_pool = pool.reshape(-1, LANES)
    pool_rows = flat_pool.shape[0]
    unit_rows = unit_share.reshape(-1, LANES)
    both = sum_over(jnp.concatenate([flat_pool, unit_rows]), ("narrow",))
    gathered, unit_rows = both[:pool_rows], both[pool_rows:]
    per_crop = jnp.repeat(crop_tokens, width // LANES)[:, None]
    gathered = gathered / per_crop
    for bit in data_bits:
        other = swap(jnp.concatenate([gathered, unit_rows]), "dp", bit)
        unit_rows = unit_rows + other[gathered.shape[0] :]
        gathered = ordered(gathered, other[: gathered.shape[0]], has_bit("dp", bit))
    unit_grad = unit_rows.reshape(unit_share.shape)
    pooled = gathered.reshape(-1, width).astype(BF16)
    all_crops, units_width = unit_grad.shape
    head_width = head_first.shape[1]
    first_act, second_act, units, embed_grad, second_low, first_low, pooled_grad = pl.pallas_call(
        head_body,
        out_shape=(
            shape((all_crops, head_width), BF16),
            shape((all_crops, head_width), BF16),
            shape((all_crops, units_width), BF16),
            shape((all_crops, units_width), F32),
            shape((all_crops, head_width), BF16),
            shape((all_crops, head_width), BF16),
            shape((all_crops, width), F32),
        ),
        in_specs=[held, held, anywhere, anywhere, anywhere, held, held, held],
        out_specs=(held,) * 7,
        scratch_shapes=[
            pltpu.VMEM(head_first.shape, BF16),
            pltpu.VMEM(head_second.shape, BF16),
            pltpu.VMEM(head_third.shape, BF16),
            pltpu.SemaphoreType.DMA((2 + head_second.shape[0] // 512,)),
        ],
        compiler_params=pltpu.CompilerParams(vmem_limit_bytes=VMEM_LIMIT),
        cost_estimate=cost(9.0),
    )(
        pooled, unit_grad, head_first, head_second, head_third,
        head_first_bias[None], head_second_bias[None], head_third_bias[None],
    )
    embed_low = embed_grad.astype(BF16)
    pooled_grad = lax.dynamic_slice_in_dim(pooled_grad, dp_index * crops, crops, 0) / crop_tokens[:, None]

    split = rows // 2
    by_chunk = lambda n: pl.BlockSpec((split, n), lambda i: (i, 0))
    out_grad, out_low, head_sums = pl.pallas_call(
        head_back_body,
        grid=(2,),
        out_shape=(shape((rows, width), F32), shape((rows, width), BF16), shape((3, width), F32)),
        in_specs=[by_chunk(width), by_chunk(width), by_chunk(1), fixed(crops, width), fixed(*norm_gains.shape)],
        out_specs=(by_chunk(width), by_chunk(width), fixed(3, width)),
        compiler_params=pltpu.CompilerParams(vmem_limit_bytes=VMEM_LIMIT),
        cost_estimate=cost(4.0),
    )(block_out, feature_cotangent, crop_of_row, pooled_grad, norm_gains)

    def by_group(part):
        return part.reshape(groups, part.shape[0] // groups, part.shape[1])

    def inner_back(act, slope, wi, wo, before=(), ending=()):
        last = bool(ending)
        n = len(wi)
        pieces = tuple(len(w) for w in wo)
        wo = [p for w in wo for p in w]
        outs = [shape((width, hidden), BF16)] * (2 * n) + [shape((n, hidden), F32), shape((rows, width), F32)]
        specs = [anywhere] * (2 * n) + [held, held if last else anywhere]
        if last:
            outs += [shape((padded_rows, width), BF16), shape((3, width), F32)]
            specs += [held, held]
        return pl.pallas_call(
            functools.partial(inner_back_body, windows, pieces, bool(before), last),
            out_shape=tuple(outs),
            in_specs=[anywhere] * (2 + 3 * n + len(wo) + len(before)) + ([anywhere, anywhere, held] if last else []),
            out_specs=tuple(specs),
            scratch_shapes=[
                low_held,
                low_held,
                pltpu.VMEM((n, rows, hidden), BF16),
                pltpu.VMEM((n, rows, hidden), BF16),
                pltpu.VMEM((n, width, hidden), BF16),
                pltpu.VMEM((n, hidden, width), BF16),
                pltpu.VMEM((n, width, hidden), BF16),
                pltpu.VMEM((n, width, hidden), BF16),
                pltpu.VMEM((n, rows, hidden), BF16),
                row_held,
                pltpu.SemaphoreType.DMA((2 + 3 * n + len(wo) + len(before) + 2 * last,)),
                pltpu.SemaphoreType.DMA((2 * n + 1,)),
            ] + ([row_held, pltpu.VMEM((rows + 16, width), F32)] if last else []),
            compiler_params=pltpu.CompilerParams(vmem_limit_bytes=VMEM_LIMIT),
            cost_estimate=cost(18.0 if last else 15.0),
        )(out_low, normed_two, *act, *slope, *wi, *wo, *before, *ending)

    o3, o1, i3, i1, sums_odd, total = inner_back([act3, act1], [slope3, slope1], [w_inner3, w_inner1], [outer3, [w_outer1]])
    got_o3, got_i3 = swap(o3, "narrow", near), swap(i3, "narrow", near)
    got_o1, got_i1 = swap(o1, "narrow", near), swap(i1, "narrow", near)
    o2, o0, i2, i0, sums_even, mixed_grad, mixed_low, mixed_sums = inner_back(
        [act2, act0], [slope2, slope0], [w_inner2, inner_weight], [outer2, [outer_weight]],
        (total,), (mixed, out_grad, norm_gains),
    )
    got_o3, got_i3, got_o1, got_i1 = after((got_o3, got_i3, got_o1, got_i1), mixed_low)
    sum_i2 = add(i2, got_i3).astype(BF16)
    keep_o2, send_o2 = halve_rows(by_group(add(o2, got_o3).astype(BF16)), share)
    keep_o0, send_o0 = halve_rows(by_group(add(o0, got_o1).astype(BF16)), share)
    got_i2 = swap(sum_i2, "narrow", far)
    got_o2 = swap(send_o2, "dp", share)
    got_o0 = swap(send_o0, "dp", share)
    sums0, sums1, sums2, sums3 = sums_even[1:2], sums_odd[1:2], sums_even[0:1], sums_odd[0:1]
    mixed_low = after(mixed_low, sum_i2, send_o0, send_o2)

    input_grads, pair_grads, input_sums = pl.pallas_call(
        functools.partial(attend_back_body, size, scale),
        grid=(padded_rows // batch,),
        out_shape=(
            shape((padded_rows, 6 * half), BF16),
            shape((PAD, 2 * pair_lanes), F32),
            shape((1, 6 * half), F32),
        ),
        in_specs=[
            by_row(width),
            fixed(count * quarter, width),
            by_row(3 * half),
            by_row(3 * half),
            by_row(pair_lanes),
            by_row(pair_lanes),
        ],
        out_specs=(by_row(6 * half), fixed(PAD, 2 * pair_lanes), fixed(1, 6 * half)),
        compiler_params=pltpu.CompilerParams(vmem_limit_bytes=VMEM_LIMIT),
        cost_estimate=cost(13.0),
    )(mixed_low, stacked_att, *qkv, *probs)

    input_sum = input_sums.reshape(2, 3, 2, quarter).transpose(0, 2, 1, 3).reshape(count, 3, quarter)
    input_sum = by_distance(input_sum, "narrow").swapaxes(0, 1).reshape(3, count * quarter)
    inner_sum = by_distance(jnp.concatenate([sums0, sums1, sums2, sums3]), "narrow").reshape(-1, width)
    ends_in = jnp.concatenate([input_sum[0:1], input_sum[2:3], inner_sum])
    packed_rows = 8 + ends_in.shape[0]
    tokens_grad, packed = call(
        functools.partial(tokens_back_body, windows),
        (shape((rows, width), F32), shape((packed_rows, width), F32)),
        (
            input_grads,
            *[v.reshape(3 * half, width) for v in stacked_in],
            tokens,
            mixed_grad,
            norm_gains,
            head_sums,
            mixed_sums,
            ends_in,
        ),
        scratch=[pltpu.VMEM((rows, width), F32)],
        us=10.0,
    )

    got_i2, got_o2, got_o0 = after((got_i2, got_o2, got_o0), tokens_grad)
    far_o = add(keep_o2, got_o2).astype(BF16)
    got_o = swap(far_o, "narrow", far)
    keep_i, send_i = halve_rows(by_group(add(add(i0, got_i1).astype(BF16), got_i2).astype(BF16)), share)
    got_i = swap(send_i, "dp", share)
    near_o = add(keep_o0, got_o0).astype(BF16)
    input_grads = after(input_grads, send_i, far_o)

    pair_shape = shape((2, width, half), BF16)
    pair_spec = pl.BlockSpec((1, width, half), lambda i: (1 - i, 0, 0))
    even_a, odd_a, even_b, odd_b = pl.pallas_call(
        weight_grad_body,
        grid=(2,),
        out_shape=(pair_shape,) * 4,
        in_specs=[
            fixed(padded_rows, width),
            fixed(padded_rows, width),
            pl.BlockSpec((padded_rows, 3 * half), lambda i: (0, 1 - i)),
            fixed(padded_rows, half),
            fixed(padded_rows, half),
        ],
        out_specs=(pair_spec,) * 4,
        compiler_params=pltpu.CompilerParams(vmem_limit_bytes=VMEM_LIMIT),
        cost_estimate=cost(12.0),
    )(padded, mixed_low, input_grads, *attended)
    got_a, got_b = swap(odd_a, "narrow", near), swap(odd_b, "narrow", near)

    got_i, got_o = after((got_i, got_o), even_a)
    mlp = jnp.concatenate([add(keep_i, got_i), add(near_o, got_o)], axis=2).astype(BF16)
    keep_m, send_m = halve_rows(mlp, data_bits[1])
    got_m = swap(send_m, "dp", data_bits[1])
    got_a, got_b = after((got_a, got_b), send_m)
    sum_a = add(even_a, got_a).astype(BF16)
    keep_b, send_b = halve_rows(add(even_b, got_b).astype(BF16).reshape(2 * groups, width // groups, half), share)
    got_a2 = swap(sum_a[1], "narrow", far)
    got_b2 = swap(send_b, "dp", share)

    pair_grads = after(pair_grads, sum_a, send_b)
    pair_grad = pair_grads.reshape(PAD, count * heads, PAD).transpose(1, 0, 2)
    table_grad = lax.dot_general(
        pair_grad.reshape(count * heads, PAD * PAD), table, (((1,), (0,)), ((), ())),
        precision=HIGH, preferred_element_type=F32,
    )
    offsets_count = table_grad.shape[1]
    table_grad = by_distance(table_grad.reshape(count, heads, offsets_count), "narrow").reshape(table_grad.shape)
    table_rows = jnp.pad(table_grad, ((0, 0), (0, 256 - offsets_count))).reshape(-1, width)
    small = jnp.concatenate([packed, table_rows])
    small_bits = [("narrow", near), ("narrow", far)] + [("dp", b) for b in data_bits]
    small_got = swap(small, *small_bits[0])

    got_a2, got_b2 = after((got_a2, got_b2), small)
    keep_a, send_a = halve_rows(by_group(add(sum_a[0], got_a2).astype(BF16)), share)
    got_a = swap(send_a, "dp", share)
    sum_b = add(keep_b, got_b2).astype(BF16).reshape(2, groups // 2, width // groups, half)
    got_b = swap(sum_b[1], "narrow", far)
    small_got, got_m = after((small_got, got_m), send_a, sum_b)
    small = small + small_got
    small_got = swap(small, *small_bits[1])
    keep_m, send_m = halve_rows(add(keep_m, got_m).astype(BF16), data_bits[2])
    got_m = swap(send_m, "dp", data_bits[2])

    units, columns_low, direction = after((units, columns_low, direction), send_m, small)
    logits = dot(units, columns_low)
    column_grad = dot_left(units, logit_cotangent)
    keep = (1 - first_epoch).astype(F32)[None, :]
    along = jnp.sum(column_grad * direction, axis=0, keepdims=True)
    gain_grad = (keep * column_inv * along)[0]
    direction_grad = (keep * prototype_gain) * (
        column_inv * column_grad - (column_inv**3 * along) * direction
    )

    got_a, got_b, small_got = after((got_a, got_b, small_got), direction_grad, logits)
    att_sum = jnp.concatenate([add(keep_a, got_a), add(sum_b[0], got_b)], axis=2).astype(BF16)
    keep_j, send_j = halve_rows(att_sum, data_bits[1])
    got_j = swap(send_j, "dp", data_bits[1])
    small = small + small_got
    small_got = swap(small, *small_bits[2])

    def own(values):
        part = values.shape[1] // groups
        return lax.dynamic_slice_in_dim(values, dp_index * part, part, 1)

    first_low, second_low, second_act, embed_grad = after((first_low, second_low, second_act, embed_grad), send_j, small)
    own_first, own_second = own(first_low), own(second_low)
    own_embed = own(embed_grad)
    first_grad = dot_left(pooled, own_first)
    second_grad = dot_left(first_act, own_second)
    third_grad = dot_left(own(second_act), embed_low)

    got_j, small_got = after((got_j, small_got), first_grad, second_grad, third_grad)
    joined = add(keep_j, got_j)
    for bit in data_bits[2:-1]:
        keep_j, send_j = halve_rows(joined.astype(BF16), bit)
        joined = add(keep_j, swap(send_j, "dp", bit))
    keep_j, send_j = halve_rows(joined.astype(BF16), data_bits[-1])
    got_j = swap(send_j, "dp", data_bits[-1])
    small = small + small_got
    small_got = swap(small, *small_bits[3])
    got_m = after(got_m, send_j)
    mlp = add(keep_m, got_m)
    for bit in data_bits[3:]:
        keep_m, send_m = halve_rows(mlp.astype(BF16), bit)
        mlp = add(keep_m, swap(send_m, "dp", bit))
    first_bias_grad = jnp.sum(own_first.astype(F32), axis=0)
    second_bias_grad = jnp.sum(own_second.astype(F32), axis=0)
    third_bias_grad = jnp.sum(own_embed, axis=0)
    small_got = after(small_got, mlp)
    small = small + small_got
    for place in small_bits[4:]:
        small = small + swap(small, *place)
    joined = add(keep_j, after(got_j, mlp))
    inner_total, outer_total = mlp[0, :, :hidden], mlp[0, :, hidden:]
    joined = joined[0]
    attend_total = joined[:, 3 * quarter :]
    input_total = jnp.stack([joined[:, i * quarter : (i + 1) * quarter] for i in range(3)])

    gain_total, offset_total, bias_total = small[0:3], small[3:8], small[8:10]
    inner_bias_total = small[10 : 10 + inner_sum.shape[0]].reshape(-1)
    table_total = small[10 + inner_sum.shape[0] :].reshape(count * heads, 256)[:, :offsets_count].T
    return (
        features,
        logits,
        tokens_grad,
        input_total,
        bias_total,
        table_total,
        attend_total.T,
        inner_total,
        inner_bias_total,
        outer_total.T,
        gain_total,
        offset_total,
        first_grad,
        first_bias_grad,
        second_grad,
        second_bias_grad,
        third_grad,
        third_bias_grad,
        direction_grad,
        gain_grad,
    )


def solution(mesh):
    placed = (
        P(("dp", "narrow"), None),
        P(None, None, "narrow"),
        P(),
        P(),
        P("narrow", None),
        P(None, "narrow"),
        P(),
        P("narrow", None),
        P(),
        P(),
        P(),
        P(),
        P(),
        P(),
        P(),
        P(),
        P(None, ("dp", "narrow")),
        P(("dp", "narrow")),
        P("dp", None),
        P(("dp", "narrow")),
        P(("dp", "narrow"), None),
        P(None, ("dp", "narrow")),
    )
    return jax.shard_map(
        shards,
        mesh=mesh,
        in_specs=placed,
        out_specs=(
            P(("dp", "narrow"), None),
            P(None, ("dp", "narrow")),
            P(("dp", "narrow"), None),
            P(None, "dp", "narrow"),
            P(),
            P(),
            P("narrow", "dp"),
            P("dp", "narrow"),
            P(),
            P("narrow", "dp"),
            P(),
            P(),
            P(None, "dp"),
            P("dp"),
            P(None, "dp"),
            P("dp"),
            P("dp", None),
            P("dp"),
            P(None, ("dp", "narrow")),
            P(("dp", "narrow")),
        ),
        check_vma=False,
    )
```

profile of v0, /device:TPU:0, one launch (start us, length us, event | category | flops | bytes accessed | tf_op | source)
XLA Modules:
  0.0 314.4 jit_solution(25713381181217969)
XLA Ops:
  1.8 3.0 collective-permute-start
  5.7 3.2 %fusion.11 = f32[64,24,64]{2,1,0:T(8,128)S(1)} fusion(f32[24,169,1]{1,0,2:T(8,128)S(1)} %reshape.412, s32[64,64]{1,0:T(8,128)S(1)} %add_select_fusion, pred[64]{0:T(512)(128)(4,1)S(1)} %iota_compare_fusion.2), kind=kOutput, calls=%fused_computation.24 | convolution fusion | flops 200151040 | bytes 425888 | tf_op jit(solution)/shard_map/dot_general | solution.py:649
  10.1 3.5 %shard_map.365.padded.x = bf16[1024,768]{1,0:T(8,128)(2,1)} custom-call(bf16[784,768]{1,0:T(8,128)(2,1)} %tokens.3, f32[3,768]{1,0:T(4,128)} %gains.5, f32[5,768]{1,0:T(8,128)} %refs_9_.2), custom_call_target="tpu_custom_call" | custom-call | bytes 11550000 | tf_op jit(solution)/shard_map/pallas_call | solution.py:40
  18.9 8.5 %shard_map.366 = (bf16[1024,1152]{1,0:T(8,128)(2,1)}, bf16[1024,768]{1,0:T(8,128)(2,1)}, bf16[1024,384]{1,0:T(8,128)(2,1)}, bf16[3,384,768]{2,1,0:T(8,128)(2,1)}) custom-call(bf16[1024,768]{1,0:T(8,128)(2,1)} %shard_map.365.padded.x, bf16[3,192,768]{2,1,0:T(8,128)(2,1)} %bitcast.181, bf16[3,192,768]{2,1,0:T(8,128)(2,1)} %copy-done.23, ...), custom_call_target="tpu_custom_call" | custom-call | bytes 29700000 | tf_op jit(solution)/shard_map/pallas_call | solution.py:674
  32.7 8.7 %shard_map.367 = (bf16[1024,1152]{1,0:T(8,128)(2,1)}, bf16[1024,768]{1,0:T(8,128)(2,1)}, bf16[1024,384]{1,0:T(8,128)(2,1)}, bf16[3,384,768]{2,1,0:T(8,128)(2,1)}) custom-call(bf16[1024,768]{1,0:T(8,128)(2,1)} %shard_map.365.padded.x, bf16[3,192,768]{2,1,0:T(8,128)(2,1)} %bitcast.171, bf16[3,192,768]{2,1,0:T(8,128)(2,1)} %copy-done.24, ...), custom_call_target="tpu_custom_call" | custom-call | bytes 29700000 | tf_op jit(solution)/shard_map/pallas_call | solution.py:674
  41.4 4.0 %collective-permute-done.7 = bf16[384,768]{1,0:T(8,128)(2,1)} collective-permute-done((bf16[384,768]{1,0:T(8,128)(2,1)}, bf16[384,768]{1,0:T(8,128)(2,1)}, u32[]{:S(2)}, u32[]{:S(2)}) %collective-permute-start.7) | collective-permute-done | bytes 589856 | tf_op jit(solution)/shard_map/ppermute | solution.py:518
  48.2 6.3 %shard_map.368 = (f32[784,768]{1,0:T(8,128)}, bf16[784,768]{1,0:T(8,128)(2,1)}, bf16[768,768]{1,0:T(8,128)(2,1)}) custom-call(bf16[1024,384]{1,0:T(8,128)(2,1)} %get-tuple-element.131.att0, bf16[1024,384]{1,0:T(8,128)(2,1)} %get-tuple-element.138.att1, bf16[192,768]{1,0:T(8,128)(2,1)} %refs_0_.1, bf16[192,768]{1,0:T(8,128)(2,1)} %collective-permute-done.5.refs_1_, ...), custom_call_target="tpu_custom_call" | custom-call | bytes 19800000 | tf_op jit(solution)/shard_map/pallas_call | solution.py:40
  54.6 7.7 %shard_map.369 = (bf16[784,768]{1,0:T(8,128)(2,1)}, bf16[784,768]{1,0:T(8,128)(2,1)}, f32[784,768]{1,0:T(8,128)}) custom-call(bf16[784,768]{1,0:T(8,128)(2,1)} %get-tuple-element.152.refs_0_.refs_1_, f32[1,1,768]{2,1,0:T(1,128)} %get-tuple-element.319.refs_1_, bf16[768,768]{1,0:T(8,128)(2,1)} %refs_7_.1, bf16[768,768]{1,0:T(8,128)(2,1)} %refs_9_.3), custom_call_target="tpu_custom_call" | custom-call | bytes 23100000 | tf_op jit(solution)/shard_map/pallas_call | solution.py:744
  65.3 7.8 %shard_map.370 = (bf16[784,768]{1,0:T(8,128)(2,1)}, bf16[784,768]{1,0:T(8,128)(2,1)}, f32[784,768]{1,0:T(8,128)}) custom-call(bf16[784,768]{1,0:T(8,128)(2,1)} %get-tuple-element.152.refs_0_.refs_1_, f32[1,1,768]{2,1,0:T(1,128)} %get-tuple-element.318.refs_1_, bf16[768,768]{1,0:T(8,128)(2,1)} %collective-permute-done.12.refs_2_.refs_7_, ...), custom_call_target="tpu_custom_call" | custom-call | bytes 23100000 | tf_op jit(solution)/shard_map/pallas_call | solution.py:744
  74.1 5.6 %collective-permute-done.11 = bf16[384,768]{1,0:T(8,128)(2,1)} collective-permute-done((bf16[384,768]{1,0:T(8,128)(2,1)}, bf16[384,768]{1,0:T(8,128)(2,1)}, u32[]{:S(2)}, u32[]{:S(2)}) %collective-permute-start.11) | collective-permute-done | bytes 589856 | tf_op jit(solution)/shard_map/ppermute | solution.py:518
  84.1 16.2 %shard_map.371 = (bf16[784,768]{1,0:T(8,128)(2,1)}, bf16[784,768]{1,0:T(8,128)(2,1)}, bf16[784,768]{1,0:T(8,128)(2,1)}, bf16[784,768]{1,0:T(8,128)(2,1)}, f32[78...) custom-call(bf16[784,768]{1,0:T(8,128)(2,1)} %get-tuple-element.152.refs_0_.refs_1_, ...), custom_call_target="tpu_custom_call" | custom-call | bytes 52800000 | tf_op jit(solution)/shard_map/pallas_call | solution.py:744
  104.1 2.4 collective-permute-done.16
  108.2 2.6 collective-permute-done.17
  112.5 2.6 collective-permute-done.18
  115.1 3.3 %collective-permute-start.19 = (f32[160,128]{1,0:T(8,128)S(1)}, f32[160,128]{1,0:T(8,128)S(1)}, u32[]{:S(2)}, u32[]{:S(2)}) collective-permute-start(f32[160,128]{1,0:T(8,128)S(1)} %pad_maximum_fusion.4), channel_id=1, source_target_pairs={{0,16},{4,20},{8,24},{12,28},{16,0},{20,4},{24,8},{28,12},{1,17},{... | collective-permute-start | bytes 245768 | tf_op jit(solution)/shard_map/ppermute | solution.py:518
  118.4 3.3 %collective-permute-done.19 = f32[160,128]{1,0:T(8,128)S(1)} collective-permute-done((f32[160,128]{1,0:T(8,128)S(1)}, f32[160,128]{1,0:T(8,128)S(1)}, u32[]{:S(2)}, u32[]{:S(2)}) %collective-permute-start.19) | collective-permute-done | bytes 81952 | tf_op jit(solution)/shard_map/ppermute | solution.py:518
  123.0 10.7 %shard_map.372 = (bf16[32,2048]{1,0:T(8,128)(2,1)}, bf16[32,2048]{1,0:T(8,128)(2,1)}, bf16[32,256]{1,0:T(8,128)(2,1)}, f32[32,256]{1,0:T(8,128)}, bf16[32,2048]{...) custom-call(bf16[32,768]{1,0:T(8,128)(2,1)} %convert_element_type.227.pooled, ...), custom_call_target="tpu_custom_call" | custom-call | bytes 29700000 | tf_op jit(solution)/shard_map/pallas_call | solution.py:799
  135.1 5.4 %shard_map.373 = (f32[784,768]{1,0:T(8,128)}, bf16[784,768]{1,0:T(8,128)(2,1)}, f32[3,768]{1,0:T(4,128)}) custom-call(f32[784,768]{1,0:T(8,128)} %get-tuple-element.161.block_out, bf16[784,768]{1,0:T(8,128)(2,1)} %cotangent.1, s32[784,1]{1,0:T(8,128)} %broadcast_in_dim.52.refs_10_.crop, f32[4,768]{1,0:T(4,128)} %dynamic-slice_divide_fusion.pooled_grad, ...), custom_call_target="tpu_custom_call" | custom-call | bytes 13200000 | tf_op jit(solution)/shard_map/pallas_call | solution.py:829
  140.5 15.7 %shard_map.374 = (bf16[768,768]{1,0:T(8,128)(2,1)}, bf16[768,768]{1,0:T(8,128)(2,1)}, bf16[768,768]{1,0:T(8,128)(2,1)}, bf16[768,768]{1,0:T(8,128)(2,1)}, f32[2,768]{1,0:T(2,128)}, /*index=5*/f32[784,768]{1,0:T(8,128)}) custom-call(bf16[784,768]{1,0:T(8,128)(2,1)} %get-tuple-element.163.refs_0_, bf16[784,768]{1,0:T(8,128)(2,1)} %get-tuple-element.152.refs_0_.refs_1_, ...), custom_call_target="tpu_custom_call" | custom-call | bytes 49500000 | tf_op jit(solution)/shard_map/pallas_call | solution.py:852
  157.3 18.9 %shard_map.375 = (bf16[768,768]{1,0:T(8,128)(2,1)}, bf16[768,768]{1,0:T(8,128)(2,1)}, bf16[768,768]{1,0:T(8,128)(2,1)}, bf16[768,768]{1,0:T(8,128)(2,1)}, f32[2,...) custom-call(bf16[784,768]{1,0:T(8,128)(2,1)} %get-tuple-element.163.refs_0_, ...), custom_call_target="tpu_custom_call" | custom-call | bytes 59400000 | tf_op jit(solution)/shard_map/pallas_call | solution.py:852
  182.6 2.8 add_convert_fusion.5
  189.1 12.3 %shard_map.376 = (bf16[1024,2304]{1,0:T(8,128)(2,1)}, f32[64,1536]{1,0:T(8,128)}, f32[1,2304]{1,0:T(1,128)}) custom-call(bf16[1024,768]{1,0:T(8,128)(2,1)} %get-tuple-element.187.low, bf16[768,768]{1,0:T(8,128)(2,1)} %get-tuple-element.188.weight, bf16[1024,1152]{1,0:T(8,128)(2,1)} %get-tuple-element.132.qkv0, bf16[1024,1152]{1,0:T(8,128)(2,1)} %get-tuple-element.141.qkv1, ...), custom_call_target="tpu_custom_call" | custom-call | bytes 42900000 | tf_op jit(solution)/shard_map/pallas_call | solution.py:892
  203.7 10.8 %shard_map.377 = (f32[784,768]{1,0:T(8,128)}, f32[14,768]{1,0:T(8,128)}) custom-call(bf16[1024,2304]{1,0:T(8,128)(2,1)} %get-tuple-element.199.grads.d, bf16[1152,768]{1,0:T(8,128)(2,1)} %bitcast.182, bf16[1152,768]{1,0:T(8,128)(2,1)} %bitcast.183, bf16[784,768]{1,0:T(8,128)(2,1)} %tokens.3, f32[784,768]{1,0:T(8,128)} %get-tuple-element.190.mixed_grad, ...), custom_call_target="tpu_custom_call" | custom-call | bytes 33000000 | tf_op jit(solution)/shard_map/pallas_call | solution.py:40
  214.5 2.3 fusion.18
  221.5 11.4 %shard_map.378 = (bf16[2,768,384]{2,1,0:T(8,128)(2,1)}, bf16[2,768,384]{2,1,0:T(8,128)(2,1)}, bf16[2,768,384]{2,1,0:T(8,128)(2,1)}, bf16[2,768,384]{2,1,0:T(8,128)(2,1)}) custom-call(bf16[1024,768]{1,0:T(8,128)(2,1)} %shard_map.365.padded.x, bf16[1024,768]{1,0:T(8,128)(2,1)} %get-tuple-element.187.low, bf16[1024,2304]{1,0:T(8,128)(2,1)} %get-tuple-element.199.grads.d, ...), custom_call_target="tpu_custom_call" | custom-call | bytes 39600000 | tf_op jit(solution)/shard_map/pallas_call | solution.py:945
  242.7 2.6 add_convert_fusion.1
  255.9 2.6 fusion.4
  260.6 9.0 %collective-permute-done.33 = bf16[768,384]{1,0:T(8,128)(2,1)} collective-permute-done((bf16[768,384]{1,0:T(8,128)(2,1)}, bf16[768,384]{1,0:T(8,128)(2,1)}, u32[]{:S(2)}, u32[]{:S(2)}) %collective-permute-start.33) | collective-permute-done | bytes 589856 | tf_op jit(solution)/shard_map/ppermute | solution.py:518
  275.0 3.1 collective-permute-start.41
  288.5 2.5 fusion.34
  300.1 3.0 collective-permute-done.42
  304.2 5.3 %collective-permute-done.43 = f32[22,768]{1,0:T(8,128)S(1)} collective-permute-done((f32[22,768]{1,0:T(8,128)S(1)}, f32[22,768]{1,0:T(8,128)S(1)}, u32[]{:S(2)}, u32[]{:S(2)}) %collective-permute-start.43) | collective-permute-done | bytes 67616 | tf_op jit(solution)/shard_map/ppermute | solution.py:518
  (298 shorter events, 105.6 us)
Async XLA Ops:
  1.8 13.2 %collective-permute-start = (bf16[288,768]{1,0:T(8,128)(2,1)S(1)}, bf16[288,768]{1,0:T(8,128)(2,1)S(1)}, u32[]{:S(2)}, u32[]{:S(2)}) collective-permute-start(bf16[288,768]{1,0:T(8,128)(2,1)S(1)} %dynamic-slice_bitcast_fusion.6), channel_id=1, source_target_pairs={{0,2},{1,3},{2,0},{3,1},{4,6},{5,7},{6,4},{7,5},{8,10},{9,11},{10,... | collective-permute-start | bytes 1327112 | tf_op jit(solution)/shard_map/ppermute | solution.py:518
  4.8 10.2 %collective-permute-start.1 = (bf16[3,192,768]{2,1,0:T(8,128)(2,1)}, bf16[3,192,768]{2,1,0:T(8,128)(2,1)S(1)}, u32[]{:S(2)}, u32[]{:S(2)}) collective-permute-start(bf16[3,192,768]{2,1,0:T(8,128)(2,1)} %bitcast.180), channel_id=1, source_target_pairs={{0,1},{1,0},{2,3},{3,2},{4,5},{5,4},{6,7},{7,6},{8,9},{9,8},{10,11... | collective-permute-start | bytes 2654216 | tf_op jit(solution)/shard_map/ppermute | solution.py:518
  15.0 12.5 %collective-permute-start.2 = (bf16[288,768]{1,0:T(8,128)(2,1)S(1)}, bf16[288,768]{1,0:T(8,128)(2,1)S(1)}, u32[]{:S(2)}, u32[]{:S(2)}) collective-permute-start(bf16[288,768]{1,0:T(8,128)(2,1)S(1)} %collective-permute-done), channel_id=1, source_target_pairs={{0,4},{4,0},{8,12},{12,8},{16,20},{20,16},{24,28},{28,24},{1,5},{5... | collective-permute-start | bytes 1327112 | tf_op jit(solution)/shard_map/ppermute | solution.py:518
  16.7 10.7 %collective-permute-start.3 = (bf16[192,768]{1,0:T(8,128)(2,1)}, bf16[192,768]{1,0:T(8,128)(2,1)S(1)}, u32[]{:S(2)}, u32[]{:S(2)}) collective-permute-start(bf16[192,768]{1,0:T(8,128)(2,1)} %refs_0_.1), channel_id=1, source_target_pairs={{0,2},{1,3},{2,0},{3,1},{4,6},{5,7},{6,4},{7,5},{8,10},{9,11},{10,... | collective-permute-start | bytes 884744 | tf_op jit(solution)/shard_map/ppermute | solution.py:518
  30.7 14.6 %collective-permute-start.7 = (bf16[384,768]{1,0:T(8,128)(2,1)}, bf16[384,768]{1,0:T(8,128)(2,1)}, u32[]{:S(2)}, u32[]{:S(2)}) collective-permute-start(bf16[384,768]{1,0:T(8,128)(2,1)} %dynamic-slice_bitcast_fusion.5), channel_id=1, source_target_pairs={{0,2},{1,3},{2,0},{3,1},{4,6},{5,7},{6,4},{7,5},{8,10},{9,11},{10,... | collective-permute-start | bytes 1769480 | tf_op jit(solution)/shard_map/ppermute | solution.py:518
  31.2 10.1 %collective-permute-start.6 = (bf16[192,768]{1,0:T(8,128)(2,1)S(1)}, bf16[192,768]{1,0:T(8,128)(2,1)}, u32[]{:S(2)}, u32[]{:S(2)}) collective-permute-start(bf16[192,768]{1,0:T(8,128)(2,1)S(1)} %copy-done.29), channel_id=1, source_target_pairs={{0,1},{1,0},{2,3},{3,2},{4,5},{5,4},{6,7},{7,6},{8,9},{9,8},{10,11... | collective-permute-start | bytes 884744 | tf_op jit(solution)/shard_map/ppermute | solution.py:518
  31.2 17.0 %collective-permute-start.5 = (bf16[192,768]{1,0:T(8,128)(2,1)}, bf16[192,768]{1,0:T(8,128)(2,1)}, u32[]{:S(2)}, u32[]{:S(2)}) collective-permute-start(bf16[192,768]{1,0:T(8,128)(2,1)} %refs_0_.1), channel_id=1, source_target_pairs={{0,1},{1,0},{2,3},{3,2},{4,5},{5,4},{6,7},{7,6},{8,9},{9,8},{10,11... | collective-permute-start | bytes 884744 | tf_op jit(solution)/shard_map/ppermute | solution.py:518
  31.8 33.5 %collective-permute-start.12 = (bf16[768,768]{1,0:T(8,128)(2,1)S(1)}, bf16[768,768]{1,0:T(8,128)(2,1)}, u32[]{:S(2)}, u32[]{:S(2)}) collective-permute-start(bf16[768,768]{1,0:T(8,128)(2,1)S(1)} %copy-done.6), channel_id=1, source_target_pairs={{0,1},{1,0},{2,3},{3,2},{4,5},{5,4},{6,7},{7,6},{8,9},{9,8},{10,11... | collective-permute-start | bytes 3538952 | tf_op jit(solution)/shard_map/ppermute | solution.py:518
  31.8 33.5 %collective-permute-start.13 = (bf16[768,768]{1,0:T(8,128)(2,1)}, bf16[768,768]{1,0:T(8,128)(2,1)}, u32[]{:S(2)}, u32[]{:S(2)}) collective-permute-start(bf16[768,768]{1,0:T(8,128)(2,1)} %refs_9_.3), channel_id=1, source_target_pairs={{0,1},{1,0},{2,3},{3,2},{4,5},{5,4},{6,7},{7,6},{8,9},{9,8},{10,11... | collective-permute-start | bytes 3538952 | tf_op jit(solution)/shard_map/ppermute | solution.py:518
  45.3 16.9 %collective-permute-start.9 = (bf16[384,768]{1,0:T(8,128)(2,1)}, bf16[384,768]{1,0:T(8,128)(2,1)S(1)}, u32[]{:S(2)}, u32[]{:S(2)}) collective-permute-start(bf16[384,768]{1,0:T(8,128)(2,1)} %collective-permute-done.7), channel_id=1, source_target_pairs={{0,4},{4,0},{8,12},{12,8},{16,20},{20,16},{24,28},{28,24},{1,5},{5... | collective-permute-start | bytes 1769480 | tf_op jit(solution)/shard_map/ppermute | solution.py:518
  47.0 15.3 %collective-permute-start.8 = (bf16[384,768]{1,0:T(8,128)(2,1)S(1)}, bf16[384,768]{1,0:T(8,128)(2,1)}, u32[]{:S(2)}, u32[]{:S(2)}) collective-permute-start(bf16[384,768]{1,0:T(8,128)(2,1)S(1)} %dynamic-slice_bitcast_fusion.4), channel_id=1, source_target_pairs={{0,2},{1,3},{2,0},{3,1},{4,6},{5,7},{6,4},{7,5},{8,10},{9,11},{10,... | collective-permute-start | bytes 1769480 | tf_op jit(solution)/shard_map/ppermute | solution.py:518
  63.5 16.1 %collective-permute-start.10 = (bf16[768,768]{1,0:T(8,128)(2,1)S(1)}, bf16[768,768]{1,0:T(8,128)(2,1)}, u32[]{:S(2)}, u32[]{:S(2)}) collective-permute-start(bf16[768,768]{1,0:T(8,128)(2,1)S(1)} %pad_maximum_fusion.refs_2_.refs_6_), channel_id=1, source_target_pairs={{0,1},{1,0},{2,3},{3,2},{4,5},{5,4},{6,7},{7,6},{8,9},{9,8},{10,11... | collective-permute-start | bytes 3538952 | tf_op jit(solution)/shard_map/ppermute | solution.py:518
  63.6 16.1 %collective-permute-start.11 = (bf16[384,768]{1,0:T(8,128)(2,1)}, bf16[384,768]{1,0:T(8,128)(2,1)}, u32[]{:S(2)}, u32[]{:S(2)}) collective-permute-start(bf16[384,768]{1,0:T(8,128)(2,1)} %collective-permute-done.8), channel_id=1, source_target_pairs={{0,8},{4,12},{8,0},{12,4},{16,24},{20,28},{24,16},{28,20},{1,9},{5... | collective-permute-start | bytes 1769480 | tf_op jit(solution)/shard_map/ppermute | solution.py:518
  156.2 21.1 %collective-permute-start.20 = (bf16[768,768]{1,0:T(8,128)(2,1)}, bf16[768,768]{1,0:T(8,128)(2,1)}, u32[]{:S(2)}, u32[]{:S(2)}) collective-permute-start(bf16[768,768]{1,0:T(8,128)(2,1)} %get-tuple-element.175), channel_id=1, source_target_pairs={{0,1},{1,0},{2,3},{3,2},{4,5},{5,4},{6,7},{7,6},{8,9},{9,8},{10,11... | collective-permute-start | bytes 3538952 | tf_op jit(solution)/shard_map/ppermute | solution.py:518
  156.3 21.0 %collective-permute-start.21 = (bf16[768,768]{1,0:T(8,128)(2,1)}, bf16[768,768]{1,0:T(8,128)(2,1)}, u32[]{:S(2)}, u32[]{:S(2)}) collective-permute-start(bf16[768,768]{1,0:T(8,128)(2,1)} %get-tuple-element.176), channel_id=1, source_target_pairs={{0,1},{1,0},{2,3},{3,2},{4,5},{5,4},{6,7},{7,6},{8,9},{9,8},{10,11... | collective-permute-start | bytes 3538952 | tf_op jit(solution)/shard_map/ppermute | solution.py:518
  156.8 20.5 %collective-permute-start.22 = (bf16[768,768]{1,0:T(8,128)(2,1)}, bf16[768,768]{1,0:T(8,128)(2,1)S(1)}, u32[]{:S(2)}, u32[]{:S(2)}) collective-permute-start(bf16[768,768]{1,0:T(8,128)(2,1)} %get-tuple-element.177), channel_id=1, source_target_pairs={{0,1},{1,0},{2,3},{3,2},{4,5},{5,4},{6,7},{7,6},{8,9},{9,8},{10,11... | collective-permute-start | bytes 3538952 | tf_op jit(solution)/shard_map/ppermute | solution.py:518
  156.8 20.5 %collective-permute-start.23 = (bf16[768,768]{1,0:T(8,128)(2,1)}, bf16[768,768]{1,0:T(8,128)(2,1)}, u32[]{:S(2)}, u32[]{:S(2)}) collective-permute-start(bf16[768,768]{1,0:T(8,128)(2,1)} %get-tuple-element.178), channel_id=1, source_target_pairs={{0,1},{1,0},{2,3},{3,2},{4,5},{5,4},{6,7},{7,6},{8,9},{9,8},{10,11... | collective-permute-start | bytes 3538952 | tf_op jit(solution)/shard_map/ppermute | solution.py:518
  181.1 33.3 %collective-permute-start.25 = (bf16[4,96,768]{2,1,0:T(8,128)(2,1)}, bf16[4,96,768]{2,1,0:T(8,128)(2,1)}, u32[]{:S(2)}, u32[]{:S(2)}) collective-permute-start(bf16[4,96,768]{2,1,0:T(8,128)(2,1)} %dynamic-slice_bitcast_fusion.3), channel_id=1, source_target_pairs={{0,4},{4,0},{8,12},{12,8},{16,20},{20,16},{24,28},{28,24},{1,5},{5... | collective-permute-start | bytes 1769480 | tf_op jit(solution)/shard_map/ppermute | solution.py:518
  185.4 29.1 %collective-permute-start.24 = (bf16[768,768]{1,0:T(8,128)(2,1)}, bf16[768,768]{1,0:T(8,128)(2,1)}, u32[]{:S(2)}, u32[]{:S(2)}) collective-permute-start(bf16[768,768]{1,0:T(8,128)(2,1)} %add_convert_fusion.5), channel_id=1, source_target_pairs={{0,2},{1,3},{2,0},{3,1},{4,6},{5,7},{6,4},{7,5},{8,10},{9,11},{10,... | collective-permute-start | bytes 3538952 | tf_op jit(solution)/shard_map/ppermute | solution.py:518
  188.1 26.4 %collective-permute-start.26 = (bf16[4,96,768]{2,1,0:T(8,128)(2,1)}, bf16[4,96,768]{2,1,0:T(8,128)(2,1)S(1)}, u32[]{:S(2)}, u32[]{:S(2)}) collective-permute-start(bf16[4,96,768]{2,1,0:T(8,128)(2,1)} %dynamic-slice_bitcast_fusion.2), channel_id=1, source_target_pairs={{0,4},{4,0},{8,12},{12,8},{16,20},{20,16},{24,28},{28,24},{1,5},{5... | collective-permute-start | bytes 1769480 | tf_op jit(solution)/shard_map/ppermute | solution.py:518
  219.8 15.1 %collective-permute-start.28 = (bf16[4,96,768]{2,1,0:T(8,128)(2,1)}, bf16[4,96,768]{2,1,0:T(8,128)(2,1)}, u32[]{:S(2)}, u32[]{:S(2)}) collective-permute-start(bf16[4,96,768]{2,1,0:T(8,128)(2,1)} %fusion.18), channel_id=1, source_target_pairs={{0,2},{1,3},{2,0},{3,1},{4,6},{5,7},{6,4},{7,5},{8,10},{9,11},{10,... | collective-permute-start | bytes 1769480 | tf_op jit(solution)/shard_map/ppermute | solution.py:518
  220.4 14.8 %collective-permute-start.27 = (bf16[4,96,768]{2,1,0:T(8,128)(2,1)}, bf16[4,96,768]{2,1,0:T(8,128)(2,1)}, u32[]{:S(2)}, u32[]{:S(2)}) collective-permute-start(bf16[4,96,768]{2,1,0:T(8,128)(2,1)} %dynamic-slice_bitcast_fusion.1), channel_id=1, source_target_pairs={{0,4},{4,0},{8,12},{12,8},{16,20},{20,16},{24,28},{28,24},{1,5},{5... | collective-permute-start | bytes 1769480 | tf_op jit(solution)/shard_map/ppermute | solution.py:518
  238.6 33.7 %collective-permute-start.32 = (bf16[2,96,1536]{2,1,0:T(8,128)(2,1)}, bf16[2,96,1536]{2,1,0:T(8,128)(2,1)}, u32[]{:S(2)}, u32[]{:S(2)}) collective-permute-start(bf16[2,96,1536]{2,1,0:T(8,128)(2,1)} %fusion.21), channel_id=1, source_target_pairs={{0,8},{4,12},{8,0},{12,4},{16,24},{20,28},{24,16},{28,20},{1,9},{5... | collective-permute-start | bytes 1769480 | tf_op jit(solution)/shard_map/ppermute | solution.py:518
  245.2 15.3 %collective-permute-start.34 = (bf16[8,96,384]{2,1,0:T(8,128)(2,1)}, bf16[8,96,384]{2,1,0:T(8,128)(2,1)}, u32[]{:S(2)}, u32[]{:S(2)}) collective-permute-start(bf16[8,96,384]{2,1,0:T(8,128)(2,1)} %dynamic-slice_bitcast_fusion), channel_id=1, source_target_pairs={{0,4},{4,0},{8,12},{12,8},{16,20},{20,16},{24,28},{28,24},{1,5},{5... | collective-permute-start | bytes 1769480 | tf_op jit(solution)/shard_map/ppermute | solution.py:518
  254.6 15.0 %collective-permute-start.33 = (bf16[768,384]{1,0:T(8,128)(2,1)}, bf16[768,384]{1,0:T(8,128)(2,1)}, u32[]{:S(2)}, u32[]{:S(2)}) collective-permute-start(bf16[768,384]{1,0:T(8,128)(2,1)} %slice_bitcast_fusion), channel_id=1, source_target_pairs={{0,2},{1,3},{2,0},{3,1},{4,6},{5,7},{6,4},{7,5},{8,10},{9,11},{10,... | collective-permute-start | bytes 1769480 | tf_op jit(solution)/shard_map/ppermute | solution.py:518
  258.5 13.7 %collective-permute-start.31 = (f32[22,768]{1,0:T(8,128)S(1)}, f32[22,768]{1,0:T(8,128)S(1)}, u32[]{:S(2)}, u32[]{:S(2)}) collective-permute-start(f32[22,768]{1,0:T(8,128)S(1)} %pad_maximum_fusion.5), channel_id=1, source_target_pairs={{0,1},{1,0},{2,3},{3,2},{4,5},{5,4},{6,7},{7,6},{8,9},{9,8},{10,11... | collective-permute-start | bytes 202760 | tf_op jit(solution)/shard_map/ppermute | solution.py:518
  271.0 15.1 %collective-permute-start.35 = (bf16[4,96,384]{2,1,0:T(8,128)(2,1)S(1)}, bf16[4,96,384]{2,1,0:T(8,128)(2,1)S(1)}, u32[]{:S(2)}, u32[]{:S(2)}) collective-permute-start(bf16[4,96,384]{2,1,0:T(8,128)(2,1)S(1)} %dynamic-slice_bitcast_fusion.7), channel_id=1, source_target_pairs={{0,4},{4,0},{8,12},{12,8},{16,20},{20,16},{24,28},{28,24},{1,5},{5... | collective-permute-start | bytes 884744 | tf_op jit(solution)/shard_map/ppermute | solution.py:518
  273.6 10.4 %collective-permute-start.37 = (f32[22,768]{1,0:T(8,128)S(1)}, f32[22,768]{1,0:T(8,128)S(1)}, u32[]{:S(2)}, u32[]{:S(2)}) collective-permute-start(f32[22,768]{1,0:T(8,128)S(1)} %fusion.47), channel_id=1, source_target_pairs={{0,2},{1,3},{2,0},{3,1},{4,6},{5,7},{6,4},{7,5},{8,10},{9,11},{10,... | collective-permute-start | bytes 202760 | tf_op jit(solution)/shard_map/ppermute | solution.py:518
  275.0 25.0 %collective-permute-start.41 = (bf16[1,96,1536]{2,1,0:T(8,128)(2,1)S(1)}, bf16[1,96,1536]{2,1,0:T(8,128)(2,1)S(1)}, u32[]{:S(2)}, u32[]{:S(2)}) collective-permute-start(bf16[1,96,1536]{2,1,0:T(8,128)(2,1)S(1)} %constant_dynamic-slice_fusion.1), channel_id=1, source_target_pairs={{0,16},{4,20},{8,24},{12,28},{16,0},{20,4},{24,8},{28,12},{1,17},{... | collective-permute-start | bytes 884744 | tf_op jit(solution)/shard_map/ppermute | solution.py:518
  286.3 11.4 %collective-permute-start.39 = (f32[22,768]{1,0:T(8,128)S(1)}, f32[22,768]{1,0:T(8,128)S(1)}, u32[]{:S(2)}, u32[]{:S(2)}) collective-permute-start(f32[22,768]{1,0:T(8,128)S(1)} %add.320), channel_id=1, source_target_pairs={{0,4},{4,0},{8,12},{12,8},{16,20},{20,16},{24,28},{28,24},{1,5},{5... | collective-permute-start | bytes 202760 | tf_op jit(solution)/shard_map/ppermute | solution.py:518
  287.5 10.3 %collective-permute-start.38 = (bf16[2,96,768]{2,1,0:T(8,128)(2,1)S(1)}, bf16[2,96,768]{2,1,0:T(8,128)(2,1)S(1)}, u32[]{:S(2)}, u32[]{:S(2)}) collective-permute-start(bf16[2,96,768]{2,1,0:T(8,128)(2,1)S(1)} %fusion.27), channel_id=1, source_target_pairs={{0,8},{4,12},{8,0},{12,4},{16,24},{20,28},{24,16},{28,20},{1,9},{5... | collective-permute-start | bytes 884744 | tf_op jit(solution)/shard_map/ppermute | solution.py:518
  299.1 13.5 %collective-permute-start.40 = (bf16[1,96,768]{2,1,0:T(8,128)(2,1)S(1)}, bf16[1,96,768]{2,1,0:T(8,128)(2,1)S(1)}, u32[]{:S(2)}, u32[]{:S(2)}) collective-permute-start(bf16[1,96,768]{2,1,0:T(8,128)(2,1)S(1)} %constant_dynamic-slice_fusion), channel_id=1, source_target_pairs={{0,16},{4,20},{8,24},{12,28},{16,0},{20,4},{24,8},{28,12},{1,17},{... | collective-permute-start | bytes 442376 | tf_op jit(solution)/shard_map/ppermute | solution.py:518
  (52 other events, 316.4 us)
where the time goes:
time: 321 us; the launch traced here: 314 us
  Pallas kernels  144 us (45%)
  waiting for transfers between devices  46.2 us (14%)
  starting transfers between devices  40.1 us (12%)
  other arithmetic  34.5 us (11%)
  local copies, waits for them, and re-layouts  34 us (11%)
  matrix products  13.7 us (4%)
    ppermute x44, waiting for transfers between devices, swap(): lax.ppermute(values, axis, [(i, i ^ bit) for i in range(lax.axis_size(axi...  46.2 us
    ppermute x44, starting transfers between devices, swap(): lax.ppermute(values, axis, [(i, i ^ bit) for i in range(lax.axis_size(axi...  40.1 us
    pallas_call x2, Pallas kernels, inner_back(): pl.pallas_call(functools.partial(inner_back_body, windows, pieces, bool(b...  34.6 us
    pallas_call x3, Pallas kernels, inner_call(): pl.pallas_call(functools.partial(inner_body, n, pieces, bool(before), las...  31.7 us
    pallas_call x3, Pallas kernels, call(): pl.pallas_call(body, out_shape=outs, in_specs=[pl.BlockSpec(memory_space=...  20.7 us
    pallas_call x2, Pallas kernels, attend(): pl.pallas_call(functools.partial(attend_body, size, scale), grid=(padded_...  17.2 us
    pallas_call x1, Pallas kernels, shards(): pl.pallas_call(functools.partial(attend_back_body, size, scale), grid=(pa...  12.3 us
    pallas_call x1, Pallas kernels, shards(): pl.pallas_call(weight_grad_body, grid=(2,), out_shape=(pair_shape,) * 4,...  11.4 us
  transfers between devices with their start and end apart: 44, of which 16 were waited for; matrix products, arithmetic and copies ran while one was open for 19% of the time, Pallas kernels for 31%

commit v1 on v0

--- a/solution.py
+++ b/solution.py
@@ -514,6 +514,29 @@
     packed[8 : 8 + ends.shape[0], :] = ends[...]
 
 
+def prototype_body(units, columns, cotangent, direction, inv, gain, flags, logits, direction_grad, gain_grad):
+    logits[...] = dot(units[...], columns[...])
+    grad = dot_left(units[...], cotangent[...])
+    keep = (1 - flags[...]).astype(F32)
+    value = direction[...].astype(F32)
+    along = jnp.sum(grad * value, axis=0, keepdims=True)
+    scale = inv[...]
+    gain_grad[...] = keep * scale * along
+    direction_grad[...] = (keep * gain[...]) * (scale * grad - (scale * scale * scale * along) * value)
+
+
+def head_grads_body(
+    pooled, first_act, second_act, first_low, second_low, embed_low, embed_grad,
+    first_grad, second_grad, third_grad, first_bias, second_bias, third_bias,
+):
+    first_grad[...] = dot_left(pooled[...], first_low[...])
+    second_grad[...] = dot_left(first_act[...], second_low[...])
+    third_grad[...] = dot_left(second_act[...], embed_low[...])
+    first_bias[...] = jnp.sum(first_low[...].astype(F32), axis=0, keepdims=True)
+    second_bias[...] = jnp.sum(second_low[...].astype(F32), axis=0, keepdims=True)
+    third_bias[...] = jnp.sum(embed_grad[...], axis=0, keepdims=True)
+
+
 def swap(values, axis, bit):
     return lax.ppermute(values, axis, [(i, i ^ bit) for i in range(lax.axis_size(axis))])
 
@@ -566,6 +589,13 @@
     return lax.dynamic_index_in_dim(parts, 2 * piece + lax.axis_index("dp") // share % 2, 0, keepdims=False)
 
 
+def rows_by_bit(values, bit, own):
+    groups, rows, columns = values.shape
+    folded = values.reshape(groups // 2, 2, rows, columns)
+    mine = lax.axis_index("dp") // bit % 2
+    return lax.dynamic_index_in_dim(folded, mine if own else 1 - mine, 1, keepdims=False)
+
+
 def halve_rows(values, bit):
     groups, rows, columns = values.shape
     folded = values.reshape(groups // 2, 2, rows, columns)
@@ -579,7 +609,7 @@
     return kept.astype(F32) + got.astype(F32)
 
 
-def offset_table():
+def offset_table(columns):
     places = jnp.arange(PAD, dtype=jnp.int32)
     row_of = places // SIDE
     col_of = places % SIDE
@@ -588,7 +618,7 @@
     )
     inside = (places[:, None] < SPOTS) & (places[None, :] < SPOTS)
     offset = jnp.where(inside, offset, -1)
-    entries = jnp.arange((2 * SIDE - 1) ** 2, dtype=jnp.int32)
+    entries = jnp.arange(columns, dtype=jnp.int32)
     return (offset.reshape(-1)[:, None] == entries[None, :]).astype(F32)
 
 
@@ -644,7 +674,8 @@
     bias_in = by_distance(input_bias.reshape(2, count, quarter).swapaxes(0, 1), "narrow")
     bias_in = bias_in.swapaxes(0, 1).reshape(2, count * quarter)
     bias_inner = by_distance(inner_bias.reshape(count, 1, hidden), "narrow")
-    table = offset_table()
+    offsets_count = position_bias.shape[0]
+    table = offset_table(offsets_count)
     turned = by_distance(position_bias.T.reshape(count, heads, -1), "narrow").reshape(count * heads, -1)
     spread = jnp.dot(table, turned.T, precision=HIGH, preferred_element_type=F32)
     spread = spread.reshape(PAD, PAD, count * heads).transpose(0, 2, 1)
@@ -821,7 +852,10 @@
         pooled, unit_grad, head_first, head_second, head_third,
         head_first_bias[None], head_second_bias[None], head_third_bias[None],
     )
-    embed_low = embed_grad.astype(BF16)
+    def own(values):
+        part = values.shape[1] // groups
+        return lax.dynamic_slice_in_dim(values, dp_index * part, part, 1)
+
     pooled_grad = lax.dynamic_slice_in_dim(pooled_grad, dp_index * crops, crops, 0) / crop_tokens[:, None]
 
     split = rows // 2
@@ -880,14 +914,23 @@
         (total,), (mixed, out_grad, norm_gains),
     )
     got_o3, got_i3, got_o1, got_i1 = after((got_o3, got_i3, got_o1, got_i1), mixed_low)
-    sum_i2 = add(i2, got_i3).astype(BF16)
-    keep_o2, send_o2 = halve_rows(by_group(add(o2, got_o3).astype(BF16)), share)
-    keep_o0, send_o0 = halve_rows(by_group(add(o0, got_o1).astype(BF16)), share)
-    got_i2 = swap(sum_i2, "narrow", far)
+    grouped = lambda *parts: [by_group(p) for p in parts]
+    o0, o1, o2, o3, i0, i1, i2, i3 = grouped(o0, got_o1, o2, got_o3, i0, got_i1, i2, got_i3)
+
+    def halved(own, first, *more):
+        total = rows_by_bit(first, share, own).astype(F32)
+        for part in more:
+            total = total + rows_by_bit(part, share, own).astype(F32)
+        return total
+
+    def rounded(value):
+        return value.astype(BF16)
+
+    send_i2 = rounded(halved(False, i2, i3))
+    send_o2 = rounded(halved(False, o2, o3))
+    got_i2s = swap(send_i2, "narrow", far)
     got_o2 = swap(send_o2, "dp", share)
-    got_o0 = swap(send_o0, "dp", share)
-    sums0, sums1, sums2, sums3 = sums_even[1:2], sums_odd[1:2], sums_even[0:1], sums_odd[0:1]
-    mixed_low = after(mixed_low, sum_i2, send_o0, send_o2)
+    mixed_low = after(mixed_low, send_i2, send_o2)
 
     input_grads, pair_grads, input_sums = pl.pallas_call(
         functools.partial(attend_back_body, size, scale),
@@ -910,35 +953,17 @@
         cost_estimate=cost(13.0),
     )(mixed_low, stacked_att, *qkv, *probs)
 
-    input_sum = input_sums.reshape(2, 3, 2, quarter).transpose(0, 2, 1, 3).reshape(count, 3, quarter)
-    input_sum = by_distance(input_sum, "narrow").swapaxes(0, 1).reshape(3, count * quarter)
-    inner_sum = by_distance(jnp.concatenate([sums0, sums1, sums2, sums3]), "narrow").reshape(-1, width)
-    ends_in = jnp.concatenate([input_sum[0:1], input_sum[2:3], inner_sum])
-    packed_rows = 8 + ends_in.shape[0]
-    tokens_grad, packed = call(
-        functools.partial(tokens_back_body, windows),
-        (shape((rows, width), F32), shape((packed_rows, width), F32)),
-        (
-            input_grads,
-            *[v.reshape(3 * half, width) for v in stacked_in],
-            tokens,
-            mixed_grad,
-            norm_gains,
-            head_sums,
-            mixed_sums,
-            ends_in,
-        ),
-        scratch=[pltpu.VMEM((rows, width), F32)],
-        us=10.0,
-    )
-
-    got_i2, got_o2, got_o0 = after((got_i2, got_o2, got_o0), tokens_grad)
-    far_o = add(keep_o2, got_o2).astype(BF16)
-    got_o = swap(far_o, "narrow", far)
-    keep_i, send_i = halve_rows(by_group(add(add(i0, got_i1).astype(BF16), got_i2).astype(BF16)), share)
-    got_i = swap(send_i, "dp", share)
-    near_o = add(keep_o0, got_o0).astype(BF16)
-    input_grads = after(input_grads, send_i, far_o)
+    pair_grad = pair_grads.reshape(PAD, count * heads, PAD).transpose(1, 0, 2)
+    table_grad = lax.dot_general(
+        pair_grad.reshape(count * heads, PAD * PAD), offset_table(256), (((1,), (0,)), ((), ())),
+        precision=HIGH, preferred_element_type=F32,
+    )
+    got_i2s, got_o2, i2, i3, o0, o1 = after((got_i2s, got_o2, i2, i3, o0, o1), table_grad)
+    send_i2 = rounded(halved(True, i2, i3))
+    send_o0 = rounded(halved(False, o0, o1))
+    got_i2k = swap(send_i2, "narrow", far)
+    got_o0 = swap(send_o0, "dp", share)
+    weight_rows = after(input_grads, send_i2, send_o0, got_i2s, got_o2)
 
     pair_shape = shape((2, width, half), BF16)
     pair_spec = pl.BlockSpec((1, width, half), lambda i: (1 - i, 0, 0))
@@ -956,90 +981,119 @@
         out_specs=(pair_spec,) * 4,
         compiler_params=pltpu.CompilerParams(vmem_limit_bytes=VMEM_LIMIT),
         cost_estimate=cost(12.0),
-    )(padded, mixed_low, input_grads, *attended)
+    )(padded, mixed_low, weight_rows, *attended)
+
+    got_i2k, got_o0, got_i2s, got_o2 = after((got_i2k, got_o0, got_i2s, got_o2), even_a)
+    far_o = rounded(halved(True, o2, o3) + got_o2.astype(F32))
+    send_i = rounded(halved(False, i0, i1) + got_i2s.astype(F32))
+    got_o = swap(far_o, "narrow", far)
+    got_i = swap(send_i, "dp", share)
+    odd_a, odd_b = after((odd_a, odd_b), far_o, send_i)
     got_a, got_b = swap(odd_a, "narrow", near), swap(odd_b, "narrow", near)
-
-    got_i, got_o = after((got_i, got_o), even_a)
-    mlp = jnp.concatenate([add(keep_i, got_i), add(near_o, got_o)], axis=2).astype(BF16)
-    keep_m, send_m = halve_rows(mlp, data_bits[1])
-    got_m = swap(send_m, "dp", data_bits[1])
-    got_a, got_b = after((got_a, got_b), send_m)
-    sum_a = add(even_a, got_a).astype(BF16)
-    keep_b, send_b = halve_rows(add(even_b, got_b).astype(BF16).reshape(2 * groups, width // groups, half), share)
-    got_a2 = swap(sum_a[1], "narrow", far)
+    sum_a = rounded(add(even_a[1], got_a[1]))
+    keep_b, send_b = halve_rows(rounded(add(even_b, got_b)).reshape(2 * groups, width // groups, half), share)
+    got_a2 = swap(sum_a, "narrow", far)
     got_b2 = swap(send_b, "dp", share)
 
-    pair_grads = after(pair_grads, sum_a, send_b)
-    pair_grad = pair_grads.reshape(PAD, count * heads, PAD).transpose(1, 0, 2)
-    table_grad = lax.dot_general(
-        pair_grad.reshape(count * heads, PAD * PAD), table, (((1,), (0,)), ((), ())),
-        precision=HIGH, preferred_element_type=F32,
-    )
-    offsets_count = table_grad.shape[1]
-    table_grad = by_distance(table_grad.reshape(count, heads, offsets_count), "narrow").reshape(table_grad.shape)
-    table_rows = jnp.pad(table_grad, ((0, 0), (0, 256 - offsets_count))).reshape(-1, width)
+    sums_even, sums_odd, input_sums = after((sums_even, sums_odd, input_sums), sum_a, send_b)
+    sums0, sums1, sums2, sums3 = sums_even[1:2], sums_odd[1:2], sums_even[0:1], sums_odd[0:1]
+    input_sum = input_sums.reshape(2, 3, 2, quarter).transpose(0, 2, 1, 3).reshape(count, 3, quarter)
+    input_sum = by_distance(input_sum, "narrow").swapaxes(0, 1).reshape(3, count * quarter)
+    inner_sum = by_distance(jnp.concatenate([sums0, sums1, sums2, sums3]), "narrow").reshape(-1, width)
+    ends_in = jnp.concatenate([input_sum[0:1], input_sum[2:3], inner_sum])
+    packed_rows = 8 + ends_in.shape[0]
+    tokens_grad, packed = call(
+        functools.partial(tokens_back_body, windows),
+        (shape((rows, width), F32), shape((packed_rows, width), F32)),
+        (
+            after(input_grads, sum_a, send_b),
+            *[v.reshape(3 * half, width) for v in stacked_in],
+            tokens,
+            mixed_grad,
+            norm_gains,
+            head_sums,
+            mixed_sums,
+            ends_in,
+        ),
+        scratch=[pltpu.VMEM((rows, width), F32)],
+        us=10.0,
+    )
+
+    table_rows = by_distance(after(table_grad, tokens_grad).reshape(count, -1, width), "narrow").reshape(-1, width)
     small = jnp.concatenate([packed, table_rows])
     small_bits = [("narrow", near), ("narrow", far)] + [("dp", b) for b in data_bits]
     small_got = swap(small, *small_bits[0])
-
-    got_a2, got_b2 = after((got_a2, got_b2), small)
-    keep_a, send_a = halve_rows(by_group(add(sum_a[0], got_a2).astype(BF16)), share)
+    got_i, got_o = after((got_i, got_o), tokens_grad)
+    mlp = rounded(jnp.concatenate([
+        halved(True, i0, i1) + got_i2k.astype(F32) + got_i.astype(F32),
+        halved(True, o0, o1) + got_o0.astype(F32) + got_o.astype(F32),
+    ], axis=2))
+    keep_m, send_m = halve_rows(mlp, data_bits[1])
+    got_m = swap(send_m, "dp", data_bits[1])
+    owned = [own(v) for v in after((first_low, second_low, second_act, embed_grad), send_m)]
+    embed_low = after(embed_grad, send_m).astype(BF16)
+    got_a2, got_b2, small_got = after((got_a2, got_b2, small_got), embed_low, *owned)
+    keep_a, send_a = halve_rows(by_group(rounded(add(even_a[0], got_a[0]) + got_a2.astype(F32))), share)
     got_a = swap(send_a, "dp", share)
-    sum_b = add(keep_b, got_b2).astype(BF16).reshape(2, groups // 2, width // groups, half)
+    sum_b = rounded(add(keep_b, got_b2)).reshape(2, groups // 2, width // groups, half)
     got_b = swap(sum_b[1], "narrow", far)
-    small_got, got_m = after((small_got, got_m), send_a, sum_b)
     small = small + small_got
     small_got = swap(small, *small_bits[1])
-    keep_m, send_m = halve_rows(add(keep_m, got_m).astype(BF16), data_bits[2])
-    got_m = swap(send_m, "dp", data_bits[2])
-
-    units, columns_low, direction = after((units, columns_low, direction), send_m, small)
-    logits = dot(units, columns_low)
-    column_grad = dot_left(units, logit_cotangent)
-    keep = (1 - first_epoch).astype(F32)[None, :]
-    along = jnp.sum(column_grad * direction, axis=0, keepdims=True)
-    gain_grad = (keep * column_inv * along)[0]
-    direction_grad = (keep * prototype_gain) * (
-        column_inv * column_grad - (column_inv**3 * along) * direction
-    )
-
-    got_a, got_b, small_got = after((got_a, got_b, small_got), direction_grad, logits)
-    att_sum = jnp.concatenate([add(keep_a, got_a), add(sum_b[0], got_b)], axis=2).astype(BF16)
+
+    own_protos = prototype_gain.shape[0]
+    logits, direction_grad, gain_grad = call(
+        prototype_body,
+        (
+            shape((all_crops, own_protos), F32),
+            shape(prototype_direction.shape, F32),
+            shape((1, own_protos), F32),
+        ),
+        (
+            after(units, send_a, sum_b, small), columns_low, logit_cotangent, prototype_direction,
+            column_inv, prototype_gain[None], first_epoch[None],
+        ),
+        us=4.0,
+    )
+
+    got_a, got_b, got_m, small_got = after((got_a, got_b, got_m, small_got), logits)
+    mlp = add(keep_m, got_m)
+    for bit in data_bits[2:-1]:
+        keep_m, send_m = halve_rows(mlp.astype(BF16), bit)
+        mlp = add(keep_m, swap(send_m, "dp", bit))
+    keep_m, send_m = halve_rows(mlp.astype(BF16), data_bits[-1])
+    got_m = swap(send_m, "dp", data_bits[-1])
+    att_sum = rounded(jnp.concatenate([add(keep_a, got_a), add(sum_b[0], got_b)], axis=2))
     keep_j, send_j = halve_rows(att_sum, data_bits[1])
     got_j = swap(send_j, "dp", data_bits[1])
     small = small + small_got
     small_got = swap(small, *small_bits[2])
 
-    def own(values):
-        part = values.shape[1] // groups
-        return lax.dynamic_slice_in_dim(values, dp_index * part, part, 1)
-
-    first_low, second_low, second_act, embed_grad = after((first_low, second_low, second_act, embed_grad), send_j, small)
-    own_first, own_second = own(first_low), own(second_low)
-    own_embed = own(embed_grad)
-    first_grad = dot_left(pooled, own_first)
-    second_grad = dot_left(first_act, own_second)
-    third_grad = dot_left(own(second_act), embed_low)
-
-    got_j, small_got = after((got_j, small_got), first_grad, second_grad, third_grad)
+    own_first, own_second, own_act, own_embed = owned
+    first_grad, second_grad, third_grad, first_bias_grad, second_bias_grad, third_bias_grad = call(
+        head_grads_body,
+        (
+            shape((pooled.shape[1], own_first.shape[1]), F32),
+            shape((first_act.shape[1], own_second.shape[1]), F32),
+            shape((own_act.shape[1], embed_low.shape[1]), F32),
+            shape((1, own_first.shape[1]), F32),
+            shape((1, own_second.shape[1]), F32),
+            shape((1, own_embed.shape[1]), F32),
+        ),
+        (after(pooled, send_m, send_j, small), first_act, own_act, own_first, own_second, embed_low, own_embed),
+        us=5.0,
+    )
+
+    got_j, got_m, small_got = after((got_j, got_m, small_got), first_grad)
+    small = small + small_got
+    small_got = swap(small, *small_bits[3])
     joined = add(keep_j, got_j)
     for bit in data_bits[2:-1]:
         keep_j, send_j = halve_rows(joined.astype(BF16), bit)
         joined = add(keep_j, swap(send_j, "dp", bit))
     keep_j, send_j = halve_rows(joined.astype(BF16), data_bits[-1])
     got_j = swap(send_j, "dp", data_bits[-1])
-    small = small + small_got
-    small_got = swap(small, *small_bits[3])
-    got_m = after(got_m, send_j)
-    mlp = add(keep_m, got_m)
-    for bit in data_bits[3:]:
-        keep_m, send_m = halve_rows(mlp.astype(BF16), bit)
-        mlp = add(keep_m, swap(send_m, "dp", bit))
-    first_bias_grad = jnp.sum(own_first.astype(F32), axis=0)
-    second_bias_grad = jnp.sum(own_second.astype(F32), axis=0)
-    third_bias_grad = jnp.sum(own_embed, axis=0)
-    small_got = after(small_got, mlp)
-    small = small + small_got
+    mlp = add(keep_m, after(got_m, send_j))
+    small = small + after(small_got, send_j)
     for place in small_bits[4:]:
         small = small + swap(small, *place)
     joined = add(keep_j, after(got_j, mlp))
@@ -1065,13 +1119,13 @@
         gain_total,
         offset_total,
         first_grad,
-        first_bias_grad,
+        first_bias_grad[0],
         second_grad,
-        second_bias_grad,
+        second_bias_grad[0],
         third_grad,
-        third_bias_grad,
+        third_bias_grad[0],
         direction_grad,
-        gain_grad,
+        gain_grad[0],
     )
 
 

time: 321 us -> 313 us (0.975)
  matrix products: 13.7 us -> 6.32 us
  Pallas kernels: 144 us -> 151 us
    dot_general x6 -> x1, matrix products: 10 us -> 2.07 us  [shards(): lax.dot_general(pair_grad.reshape(count * heads, PAD * PAD), offset_table...]
    pallas_call x3 -> x5, Pallas kernels: 20.7 us -> 27.6 us  [call(): pl.pallas_call(body, out_shape=outs, in_specs=[pl.BlockSpec(memory_space=...]
    dynamic_slice x0 -> x4, local copies, waits for them, and re-layouts: none -> 4.66 us  [own(): return lax.dynamic_slice_in_dim(values, dp_index * part, part, 1)]
    ppermute x44 -> x45, starting transfers between devices: 40.1 us -> 37.8 us  [swap(): lax.ppermute(values, axis, [(i, i ^ bit) for i in range(lax.axis_size(axi...]
    unnamed x82 -> x102, local copies, waits for them, and re-layouts: 5.96 us -> 7.33 us
    convert_element_type x11 -> x12, other arithmetic: 17.7 us -> 17.7 us  [the longest x10 17 us: rounded(): return value.astype(BF16)]
    ppermute x44 -> x45, waiting for transfers between devices: 46.2 us -> 46.3 us  [swap(): lax.ppermute(values, axis, [(i, i ^ bit) for i in range(lax.axis_size(axi...]
  transfers between devices with their start and end apart: 44 -> 45, of which waited for: 16 -> 18; matrix products, arithmetic and copies ran while one was open for 19% -> 15% of each run, Pallas kernels for 31% -> 34%
where the time goes in v1:
time: 313 us; the launch traced here: 307 us
  Pallas kernels  151 us (48%)
  waiting for transfers between devices  46.3 us (15%)
  starting transfers between devices  37.8 us (12%)
  local copies, waits for them, and re-layouts  31.9 us (10%)
  other arithmetic  31.6 us (10%)
  matrix products  6.32 us (2%)
    ppermute x45, waiting for transfers between devices, swap(): lax.ppermute(values, axis, [(i, i ^ bit) for i in range(lax.axis_size(axi...  46.3 us
    ppermute x45, starting transfers between devices, swap(): lax.ppermute(values, axis, [(i, i ^ bit) for i in range(lax.axis_size(axi...  37.8 us
    pallas_call x2, Pallas kernels, inner_back(): pl.pallas_call(functools.partial(inner_back_body, windows, pieces, bool(b...  34.8 us
    pallas_call x3, Pallas kernels, inner_call(): pl.pallas_call(functools.partial(inner_body, n, pieces, bool(before), las...  31.5 us
    pallas_call x5, Pallas kernels, call(): pl.pallas_call(body, out_shape=outs, in_specs=[pl.BlockSpec(memory_space=...  27.6 us
    pallas_call x2, Pallas kernels, attend(): pl.pallas_call(functools.partial(attend_body, size, scale), grid=(padded_...  17.2 us
    convert_element_type x10, other arithmetic, rounded(): return value.astype(BF16)  17 us
    pallas_call x1, Pallas kernels, shards(): pl.pallas_call(functools.partial(attend_back_body, size, scale), grid=(pa...  12.4 us
  transfers between devices with their start and end apart: 45, of which 18 were waited for; matrix products, arithmetic and copies ran while one was open for 15% of the time, Pallas kernels for 34%

profile of v1, /device:TPU:0, one launch (start us, length us, event | category | flops | bytes accessed | tf_op | source)
XLA Modules:
  0.0 306.8 jit_solution(4146559866735538449)
XLA Ops:
  1.7 3.0 collective-permute-start
  7.1 3.2 %fusion.12 = f32[64,24,64]{2,1,0:T(8,128)S(1)} fusion(f32[24,169,1]{1,0,2:T(8,128)S(1)} %reshape.448, s32[64,64]{1,0:T(8,128)S(1)} %add_select_fusion, pred[64]{0:T(512)(128)(4,1)S(1)} %iota_compare_fusion.3), kind=kOutput, calls=%fused_computation.18 | convolution fusion | flops 200151040 | bytes 425888 | tf_op jit(solution)/shard_map/dot_general | solution.py:680
  11.3 3.5 %shard_map.365.padded.x = bf16[1024,768]{1,0:T(8,128)(2,1)} custom-call(bf16[784,768]{1,0:T(8,128)(2,1)} %tokens.3, f32[3,768]{1,0:T(4,128)} %gains.5, f32[5,768]{1,0:T(8,128)} %refs_9_.2), custom_call_target="tpu_custom_call" | custom-call | bytes 11550000 | tf_op jit(solution)/shard_map/pallas_call | solution.py:40
  18.9 8.5 %shard_map.366 = (bf16[1024,1152]{1,0:T(8,128)(2,1)}, bf16[1024,768]{1,0:T(8,128)(2,1)}, bf16[1024,384]{1,0:T(8,128)(2,1)}, bf16[3,384,768]{2,1,0:T(8,128)(2,1)}) custom-call(bf16[1024,768]{1,0:T(8,128)(2,1)} %shard_map.365.padded.x, bf16[3,192,768]{2,1,0:T(8,128)(2,1)} %bitcast.215, bf16[3,192,768]{2,1,0:T(8,128)(2,1)} %copy-done.25, ...), custom_call_target="tpu_custom_call" | custom-call | bytes 29700000 | tf_op jit(solution)/shard_map/pallas_call | solution.py:705
  31.5 8.7 %shard_map.367 = (bf16[1024,1152]{1,0:T(8,128)(2,1)}, bf16[1024,768]{1,0:T(8,128)(2,1)}, bf16[1024,384]{1,0:T(8,128)(2,1)}, bf16[3,384,768]{2,1,0:T(8,128)(2,1)}) custom-call(bf16[1024,768]{1,0:T(8,128)(2,1)} %shard_map.365.padded.x, bf16[3,192,768]{2,1,0:T(8,128)(2,1)} %bitcast.205, bf16[3,192,768]{2,1,0:T(8,128)(2,1)} %collective-permute-done.4.far, ...), custom_call_target="tpu_custom_call" | custom-call | bytes 29700000 | tf_op jit(solution)/shard_map/pallas_call | solution.py:705
  40.2 5.1 %collective-permute-done.7 = bf16[384,768]{1,0:T(8,128)(2,1)} collective-permute-done((bf16[384,768]{1,0:T(8,128)(2,1)}, bf16[384,768]{1,0:T(8,128)(2,1)}, u32[]{:S(2)}, u32[]{:S(2)}) %collective-permute-start.7) | collective-permute-done | bytes 589856 | tf_op jit(solution)/shard_map/ppermute | solution.py:541
  49.1 6.3 %shard_map.368 = (f32[784,768]{1,0:T(8,128)}, bf16[784,768]{1,0:T(8,128)(2,1)}, bf16[768,768]{1,0:T(8,128)(2,1)}) custom-call(bf16[1024,384]{1,0:T(8,128)(2,1)} %get-tuple-element.152.att0, bf16[1024,384]{1,0:T(8,128)(2,1)} %get-tuple-element.159.att1, bf16[192,768]{1,0:T(8,128)(2,1)} %refs_0_.1, bf16[192,768]{1,0:T(8,128)(2,1)} %collective-permute-done.5.refs_1_, ...), custom_call_target="tpu_custom_call" | custom-call | bytes 19800000 | tf_op jit(solution)/shard_map/pallas_call | solution.py:40
  55.3 7.6 %shard_map.369 = (bf16[784,768]{1,0:T(8,128)(2,1)}, bf16[784,768]{1,0:T(8,128)(2,1)}, f32[784,768]{1,0:T(8,128)}) custom-call(bf16[784,768]{1,0:T(8,128)(2,1)} %get-tuple-element.173.refs_0_.refs_1_, f32[1,1,768]{2,1,0:T(1,128)} %get-tuple-element.379.refs_1_, bf16[768,768]{1,0:T(8,128)(2,1)} %refs_7_.1, bf16[768,768]{1,0:T(8,128)(2,1)} %refs_9_.3), custom_call_target="tpu_custom_call" | custom-call | bytes 23100000 | tf_op jit(solution)/shard_map/pallas_call | solution.py:775
  66.1 7.7 %shard_map.370 = (bf16[784,768]{1,0:T(8,128)(2,1)}, bf16[784,768]{1,0:T(8,128)(2,1)}, f32[784,768]{1,0:T(8,128)}) custom-call(bf16[784,768]{1,0:T(8,128)(2,1)} %get-tuple-element.173.refs_0_.refs_1_, f32[1,1,768]{2,1,0:T(1,128)} %get-tuple-element.378.refs_1_, bf16[768,768]{1,0:T(8,128)(2,1)} %collective-permute-done.12.refs_2_.refs_7_, ...), custom_call_target="tpu_custom_call" | custom-call | bytes 23100000 | tf_op jit(solution)/shard_map/pallas_call | solution.py:775
  76.0 4.5 %collective-permute-done.11 = bf16[384,768]{1,0:T(8,128)(2,1)} collective-permute-done((bf16[384,768]{1,0:T(8,128)(2,1)}, bf16[384,768]{1,0:T(8,128)(2,1)}, u32[]{:S(2)}, u32[]{:S(2)}) %collective-permute-start.11) | collective-permute-done | bytes 589856 | tf_op jit(solution)/shard_map/ppermute | solution.py:541
  85.8 16.3 %shard_map.371 = (bf16[784,768]{1,0:T(8,128)(2,1)}, bf16[784,768]{1,0:T(8,128)(2,1)}, bf16[784,768]{1,0:T(8,128)(2,1)}, bf16[784,768]{1,0:T(8,128)(2,1)}, f32[78...) custom-call(bf16[784,768]{1,0:T(8,128)(2,1)} %get-tuple-element.173.refs_0_.refs_1_, ...), custom_call_target="tpu_custom_call" | custom-call | bytes 52800000 | tf_op jit(solution)/shard_map/pallas_call | solution.py:775
  109.2 3.2 %collective-permute-done.17 = f32[88,128]{1,0:T(8,128)S(1)} collective-permute-done((f32[88,128]{1,0:T(8,128)S(1)}, f32[88,128]{1,0:T(8,128)S(1)}, u32[]{:S(2)}, u32[]{:S(2)}) %collective-permute-start.17) | collective-permute-done | bytes 45088 | tf_op jit(solution)/shard_map/ppermute | solution.py:541
  114.1 2.6 collective-permute-done.18
  116.8 3.3 %collective-permute-start.19 = (f32[160,128]{1,0:T(8,128)S(1)}, f32[160,128]{1,0:T(8,128)S(1)}, u32[]{:S(2)}, u32[]{:S(2)}) collective-permute-start(f32[160,128]{1,0:T(8,128)S(1)} %pad_maximum_fusion.4), channel_id=1, source_target_pairs={{0,16},{4,20},{8,24},{12,28},{16,0},{20,4},{24,8},{28,12},{1,17},{... | collective-permute-start | bytes 245768 | tf_op jit(solution)/shard_map/ppermute | solution.py:541
  120.0 3.3 %collective-permute-done.19 = f32[160,128]{1,0:T(8,128)S(1)} collective-permute-done((f32[160,128]{1,0:T(8,128)S(1)}, f32[160,128]{1,0:T(8,128)S(1)}, u32[]{:S(2)}, u32[]{:S(2)}) %collective-permute-start.19) | collective-permute-done | bytes 81952 | tf_op jit(solution)/shard_map/ppermute | solution.py:541
  124.7 10.7 %shard_map.372 = (bf16[32,2048]{1,0:T(8,128)(2,1)}, bf16[32,2048]{1,0:T(8,128)(2,1)}, bf16[32,256]{1,0:T(8,128)(2,1)}, f32[32,256]{1,0:T(8,128)}, bf16[32,2048]{...) custom-call(bf16[32,768]{1,0:T(8,128)(2,1)} %convert_element_type.252.pooled, ...), custom_call_target="tpu_custom_call" | custom-call | bytes 29700000 | tf_op jit(solution)/shard_map/pallas_call | solution.py:830
  136.8 5.4 %shard_map.373 = (f32[784,768]{1,0:T(8,128)}, bf16[784,768]{1,0:T(8,128)(2,1)}, f32[3,768]{1,0:T(4,128)}) custom-call(f32[784,768]{1,0:T(8,128)} %get-tuple-element.182.block_out, bf16[784,768]{1,0:T(8,128)(2,1)} %cotangent.2, s32[784,1]{1,0:T(8,128)} %broadcast_in_dim.65.refs_10_.crop, f32[4,768]{1,0:T(4,128)} %dynamic-slice_divide_fusion.pooled_grad, ...), custom_call_target="tpu_custom_call" | custom-call | bytes 13200000 | tf_op jit(solution)/shard_map/pallas_call | solution.py:863
  142.2 15.7 %shard_map.374 = (bf16[768,768]{1,0:T(8,128)(2,1)}, bf16[768,768]{1,0:T(8,128)(2,1)}, bf16[768,768]{1,0:T(8,128)(2,1)}, bf16[768,768]{1,0:T(8,128)(2,1)}, f32[2,768]{1,0:T(2,128)}, /*index=5*/f32[784,768]{1,0:T(8,128)}) custom-call(bf16[784,768]{1,0:T(8,128)(2,1)} %get-tuple-element.184.refs_0_, bf16[784,768]{1,0:T(8,128)(2,1)} %get-tuple-element.173.refs_0_.refs_1_, ...), custom_call_target="tpu_custom_call" | custom-call | bytes 49500000 | tf_op jit(solution)/shard_map/pallas_call | solution.py:886
  158.9 19.1 %shard_map.375 = (bf16[768,768]{1,0:T(8,128)(2,1)}, bf16[768,768]{1,0:T(8,128)(2,1)}, bf16[768,768]{1,0:T(8,128)(2,1)}, bf16[768,768]{1,0:T(8,128)(2,1)}, f32[2,...) custom-call(bf16[784,768]{1,0:T(8,128)(2,1)} %get-tuple-element.184.refs_0_, ...), custom_call_target="tpu_custom_call" | custom-call | bytes 59400000 | tf_op jit(solution)/shard_map/pallas_call | solution.py:886
  178.2 3.4 %fusion.24 = bf16[4,96,768]{2,1,0:T(8,128)(2,1)} fusion(bf16[4,2,96,768]{3,2,1,0:T(8,128)(2,1)} %bitcast.27, s32[]{:T(128)S(6)} %select_n.489, bf16[4,2,96,768]{3,2,1,0:T(8,128)(2,1)} %bitcast.230), kind=kLoop, calls=%fused_computation.49 | loop fusion | flops 1179648 | bytes 1769476 | tf_op jit(solution)/shard_map/convert_element_type | solution.py:927
  185.6 12.4 %shard_map.376 = (bf16[1024,2304]{1,0:T(8,128)(2,1)}, f32[64,1536]{1,0:T(8,128)}, f32[1,2304]{1,0:T(1,128)}) custom-call(bf16[1024,768]{1,0:T(8,128)(2,1)} %get-tuple-element.204.low, bf16[768,768]{1,0:T(8,128)(2,1)} %get-tuple-element.205.weight, bf16[1024,1152]{1,0:T(8,128)(2,1)} %get-tuple-element.153.qkv0, bf16[1024,1152]{1,0:T(8,128)(2,1)} %get-tuple-element.162.qkv1, ...), custom_call_target="tpu_custom_call" | custom-call | bytes 42900000 | tf_op jit(solution)/shard_map/pallas_call | solution.py:935
  206.5 11.5 %shard_map.377 = (bf16[2,768,384]{2,1,0:T(8,128)(2,1)}, bf16[2,768,384]{2,1,0:T(8,128)(2,1)}, bf16[2,768,384]{2,1,0:T(8,128)(2,1)}, bf16[2,768,384]{2,1,0:T(8,128)(2,1)}) custom-call(bf16[1024,768]{1,0:T(8,128)(2,1)} %shard_map.365.padded.x, bf16[1024,768]{1,0:T(8,128)(2,1)} %get-tuple-element.204.low, bf16[1024,2304]{1,0:T(8,128)(2,1)} %get-tuple-element.227.d.grads, ...), custom_call_target="tpu_custom_call" | custom-call | bytes 39600000 | tf_op jit(solution)/shard_map/pallas_call | solution.py:970
  218.0 3.0 collective-permute-done.26
  221.0 2.2 fusion.23
  228.4 2.4 fusion.28
  235.0 10.8 %shard_map.378 = (f32[784,768]{1,0:T(8,128)}, f32[14,768]{1,0:T(8,128)}) custom-call(bf16[1024,2304]{1,0:T(8,128)(2,1)} %get-tuple-element.227.d.grads, bf16[1152,768]{1,0:T(8,128)(2,1)} %bitcast.216, bf16[1152,768]{1,0:T(8,128)(2,1)} %bitcast.217, bf16[784,768]{1,0:T(8,128)(2,1)} %tokens.3, f32[784,768]{1,0:T(8,128)} %get-tuple-element.228.mixed_grad, ...), custom_call_target="tpu_custom_call" | custom-call | bytes 33000000 | tf_op jit(solution)/shard_map/pallas_call | solution.py:40
  264.8 4.0 %shard_map.379 = (f32[32,2048]{1,0:T(8,128)}, f32[256,2048]{1,0:T(8,128)}, f32[1,2048]{1,0:T(1,128)}) custom-call(bf16[32,256]{1,0:T(8,128)(2,1)} %get-tuple-element.255.units, bf16[256,2048]{1,0:T(8,128)(2,1)} %copy-done.3, bf16[32,2048]{1,0:T(8,128)(2,1)} %cotangent.3, bf16[256,2048]{1,0:T(8,128)(2,1)} %direction.1, f32[1,2048]{1,0:T(1,128)} %bitcast.233, ...), custom_call_target="tpu_custom_call" | custom-call | bytes 13200000 | tf_op jit(solution)/shard_map/pallas_call | solution.py:40
  273.2 3.4 %collective-permute-start.40 = (bf16[1,96,1536]{2,1,0:T(8,128)(2,1)S(1)}, bf16[1,96,1536]{2,1,0:T(8,128)(2,1)S(1)}, u32[]{:S(2)}, u32[]{:S(2)}) collective-permute-start(bf16[1,96,1536]{2,1,0:T(8,128)(2,1)S(1)} %constant_dynamic-slice_fusion.5), channel_id=1, source_target_pairs={{0,16},{4,20},{8,24},{12,28},{16,0},{20,4},{24,8},{28,12},{1,17},{... | collective-permute-start | bytes 884744 | tf_op jit(solution)/shard_map/ppermute | solution.py:541
  279.3 3.0 shard_map.380
  282.4 6.6 %collective-permute-done.40 = bf16[1,96,1536]{2,1,0:T(8,128)(2,1)S(1)} collective-permute-done((bf16[1,96,1536]{2,1,0:T(8,128)(2,1)S(1)}, bf16[1,96,1536]{2,1,0:T(8,128)(2,1)S(1)}, u32[]{:S(2)}, u32[]{:S(2)}) %collective-permute-start.40) | collective-permute-done | bytes 294944 | tf_op jit(solution)/shard_map/ppermute | solution.py:541
  292.2 2.5 collective-permute-done.43
  295.7 6.3 %collective-permute-done.44 = f32[22,768]{1,0:T(8,128)S(1)} collective-permute-done((f32[22,768]{1,0:T(8,128)S(1)}, f32[22,768]{1,0:T(8,128)S(1)}, u32[]{:S(2)}, u32[]{:S(2)}) %collective-permute-start.44) | collective-permute-done | bytes 67616 | tf_op jit(solution)/shard_map/ppermute | solution.py:541
  (312 shorter events, 96.0 us)
Async XLA Ops:
  1.7 13.2 %collective-permute-start = (bf16[288,768]{1,0:T(8,128)(2,1)S(1)}, bf16[288,768]{1,0:T(8,128)(2,1)S(1)}, u32[]{:S(2)}, u32[]{:S(2)}) collective-permute-start(bf16[288,768]{1,0:T(8,128)(2,1)S(1)} %dynamic-slice_bitcast_fusion.3), channel_id=1, source_target_pairs={{0,2},{1,3},{2,0},{3,1},{4,6},{5,7},{6,4},{7,5},{8,10},{9,11},{10,... | collective-permute-start | bytes 1327112 | tf_op jit(solution)/shard_map/ppermute | solution.py:541
  4.7 10.2 %collective-permute-start.1 = (bf16[3,192,768]{2,1,0:T(8,128)(2,1)}, bf16[3,192,768]{2,1,0:T(8,128)(2,1)S(1)}, u32[]{:S(2)}, u32[]{:S(2)}) collective-permute-start(bf16[3,192,768]{2,1,0:T(8,128)(2,1)} %bitcast.214), channel_id=1, source_target_pairs={{0,1},{1,0},{2,3},{3,2},{4,5},{5,4},{6,7},{7,6},{8,9},{9,8},{10,11... | collective-permute-start | bytes 2654216 | tf_op jit(solution)/shard_map/ppermute | solution.py:541
  14.9 12.6 %collective-permute-start.2 = (bf16[288,768]{1,0:T(8,128)(2,1)S(1)}, bf16[288,768]{1,0:T(8,128)(2,1)S(1)}, u32[]{:S(2)}, u32[]{:S(2)}) collective-permute-start(bf16[288,768]{1,0:T(8,128)(2,1)S(1)} %collective-permute-done), channel_id=1, source_target_pairs={{0,4},{4,0},{8,12},{12,8},{16,20},{20,16},{24,28},{28,24},{1,5},{5... | collective-permute-start | bytes 1327112 | tf_op jit(solution)/shard_map/ppermute | solution.py:541
  16.7 10.7 %collective-permute-start.3 = (bf16[192,768]{1,0:T(8,128)(2,1)}, bf16[192,768]{1,0:T(8,128)(2,1)S(1)}, u32[]{:S(2)}, u32[]{:S(2)}) collective-permute-start(bf16[192,768]{1,0:T(8,128)(2,1)} %refs_0_.1), channel_id=1, source_target_pairs={{0,2},{1,3},{2,0},{3,1},{4,6},{5,7},{6,4},{7,5},{8,10},{9,11},{10,... | collective-permute-start | bytes 884744 | tf_op jit(solution)/shard_map/ppermute | solution.py:541
  30.1 15.3 %collective-permute-start.7 = (bf16[384,768]{1,0:T(8,128)(2,1)}, bf16[384,768]{1,0:T(8,128)(2,1)}, u32[]{:S(2)}, u32[]{:S(2)}) collective-permute-start(bf16[384,768]{1,0:T(8,128)(2,1)} %dynamic-slice_bitcast_fusion.2), channel_id=1, source_target_pairs={{0,2},{1,3},{2,0},{3,1},{4,6},{5,7},{6,4},{7,5},{8,10},{9,11},{10,... | collective-permute-start | bytes 1769480 | tf_op jit(solution)/shard_map/ppermute | solution.py:541
  30.5 9.7 %collective-permute-start.6 = (bf16[192,768]{1,0:T(8,128)(2,1)S(1)}, bf16[192,768]{1,0:T(8,128)(2,1)}, u32[]{:S(2)}, u32[]{:S(2)}) collective-permute-start(bf16[192,768]{1,0:T(8,128)(2,1)S(1)} %collective-permute-done.3.refs_2_), channel_id=1, source_target_pairs={{0,1},{1,0},{2,3},{3,2},{4,5},{5,4},{6,7},{7,6},{8,9},{9,8},{10,11... | collective-permute-start | bytes 884744 | tf_op jit(solution)/shard_map/ppermute | solution.py:541
  30.5 18.5 %collective-permute-start.5 = (bf16[192,768]{1,0:T(8,128)(2,1)}, bf16[192,768]{1,0:T(8,128)(2,1)}, u32[]{:S(2)}, u32[]{:S(2)}) collective-permute-start(bf16[192,768]{1,0:T(8,128)(2,1)} %refs_0_.1), channel_id=1, source_target_pairs={{0,1},{1,0},{2,3},{3,2},{4,5},{5,4},{6,7},{7,6},{8,9},{9,8},{10,11... | collective-permute-start | bytes 884744 | tf_op jit(solution)/shard_map/ppermute | solution.py:541
  31.0 35.1 %collective-permute-start.12 = (bf16[768,768]{1,0:T(8,128)(2,1)S(1)}, bf16[768,768]{1,0:T(8,128)(2,1)}, u32[]{:S(2)}, u32[]{:S(2)}) collective-permute-start(bf16[768,768]{1,0:T(8,128)(2,1)S(1)} %copy-done.4), channel_id=1, source_target_pairs={{0,1},{1,0},{2,3},{3,2},{4,5},{5,4},{6,7},{7,6},{8,9},{9,8},{10,11... | collective-permute-start | bytes 3538952 | tf_op jit(solution)/shard_map/ppermute | solution.py:541
  31.0 35.1 %collective-permute-start.13 = (bf16[768,768]{1,0:T(8,128)(2,1)S(1)}, bf16[768,768]{1,0:T(8,128)(2,1)}, u32[]{:S(2)}, u32[]{:S(2)}) collective-permute-start(bf16[768,768]{1,0:T(8,128)(2,1)S(1)} %copy-done.5), channel_id=1, source_target_pairs={{0,1},{1,0},{2,3},{3,2},{4,5},{5,4},{6,7},{7,6},{8,9},{9,8},{10,11... | collective-permute-start | bytes 3538952 | tf_op jit(solution)/shard_map/ppermute | solution.py:541
  45.4 17.5 %collective-permute-start.9 = (bf16[384,768]{1,0:T(8,128)(2,1)}, bf16[384,768]{1,0:T(8,128)(2,1)S(1)}, u32[]{:S(2)}, u32[]{:S(2)}) collective-permute-start(bf16[384,768]{1,0:T(8,128)(2,1)} %collective-permute-done.7), channel_id=1, source_target_pairs={{0,4},{4,0},{8,12},{12,8},{16,20},{20,16},{24,28},{28,24},{1,5},{5... | collective-permute-start | bytes 1769480 | tf_op jit(solution)/shard_map/ppermute | solution.py:541
  47.5 15.3 %collective-permute-start.8 = (bf16[384,768]{1,0:T(8,128)(2,1)}, bf16[384,768]{1,0:T(8,128)(2,1)S(1)}, u32[]{:S(2)}, u32[]{:S(2)}) collective-permute-start(bf16[384,768]{1,0:T(8,128)(2,1)} %dynamic-slice_bitcast_fusion.1), channel_id=1, source_target_pairs={{0,2},{1,3},{2,0},{3,1},{4,6},{5,7},{6,4},{7,5},{8,10},{9,11},{10,... | collective-permute-start | bytes 1769480 | tf_op jit(solution)/shard_map/ppermute | solution.py:541
  64.4 16.1 %collective-permute-start.10 = (bf16[768,768]{1,0:T(8,128)(2,1)S(1)}, bf16[768,768]{1,0:T(8,128)(2,1)}, u32[]{:S(2)}, u32[]{:S(2)}) collective-permute-start(bf16[768,768]{1,0:T(8,128)(2,1)S(1)} %pad_maximum_fusion.refs_2_.refs_6_), channel_id=1, source_target_pairs={{0,1},{1,0},{2,3},{3,2},{4,5},{5,4},{6,7},{7,6},{8,9},{9,8},{10,11... | collective-permute-start | bytes 3538952 | tf_op jit(solution)/shard_map/ppermute | solution.py:541
  64.5 16.1 %collective-permute-start.11 = (bf16[384,768]{1,0:T(8,128)(2,1)}, bf16[384,768]{1,0:T(8,128)(2,1)}, u32[]{:S(2)}, u32[]{:S(2)}) collective-permute-start(bf16[384,768]{1,0:T(8,128)(2,1)} %copy-done.26), channel_id=1, source_target_pairs={{0,8},{4,12},{8,0},{12,4},{16,24},{20,28},{24,16},{28,20},{1,9},{5... | collective-permute-start | bytes 1769480 | tf_op jit(solution)/shard_map/ppermute | solution.py:541
  157.9 20.2 %collective-permute-start.20 = (bf16[768,768]{1,0:T(8,128)(2,1)}, bf16[768,768]{1,0:T(8,128)(2,1)S(1)}, u32[]{:S(2)}, u32[]{:S(2)}) collective-permute-start(bf16[768,768]{1,0:T(8,128)(2,1)} %get-tuple-element.197), channel_id=1, source_target_pairs={{0,1},{1,0},{2,3},{3,2},{4,5},{5,4},{6,7},{7,6},{8,9},{9,8},{10,11... | collective-permute-start | bytes 3538952 | tf_op jit(solution)/shard_map/ppermute | solution.py:541
  157.9 20.2 %collective-permute-start.21 = (bf16[768,768]{1,0:T(8,128)(2,1)}, bf16[768,768]{1,0:T(8,128)(2,1)}, u32[]{:S(2)}, u32[]{:S(2)}) collective-permute-start(bf16[768,768]{1,0:T(8,128)(2,1)} %get-tuple-element.198), channel_id=1, source_target_pairs={{0,1},{1,0},{2,3},{3,2},{4,5},{5,4},{6,7},{7,6},{8,9},{9,8},{10,11... | collective-permute-start | bytes 3538952 | tf_op jit(solution)/shard_map/ppermute | solution.py:541
  158.4 19.7 %collective-permute-start.22 = (bf16[768,768]{1,0:T(8,128)(2,1)}, bf16[768,768]{1,0:T(8,128)(2,1)S(1)}, u32[]{:S(2)}, u32[]{:S(2)}) collective-permute-start(bf16[768,768]{1,0:T(8,128)(2,1)} %get-tuple-element.199), channel_id=1, source_target_pairs={{0,1},{1,0},{2,3},{3,2},{4,5},{5,4},{6,7},{7,6},{8,9},{9,8},{10,11... | collective-permute-start | bytes 3538952 | tf_op jit(solution)/shard_map/ppermute | solution.py:541
  158.5 19.6 %collective-permute-start.23 = (bf16[768,768]{1,0:T(8,128)(2,1)}, bf16[768,768]{1,0:T(8,128)(2,1)S(1)}, u32[]{:S(2)}, u32[]{:S(2)}) collective-permute-start(bf16[768,768]{1,0:T(8,128)(2,1)} %get-tuple-element.200), channel_id=1, source_target_pairs={{0,1},{1,0},{2,3},{3,2},{4,5},{5,4},{6,7},{7,6},{8,9},{9,8},{10,11... | collective-permute-start | bytes 3538952 | tf_op jit(solution)/shard_map/ppermute | solution.py:541
  181.6 20.1 %collective-permute-start.24 = (bf16[4,96,768]{2,1,0:T(8,128)(2,1)}, bf16[4,96,768]{2,1,0:T(8,128)(2,1)}, u32[]{:S(2)}, u32[]{:S(2)}) collective-permute-start(bf16[4,96,768]{2,1,0:T(8,128)(2,1)} %fusion.24), channel_id=1, source_target_pairs={{0,2},{1,3},{2,0},{3,1},{4,6},{5,7},{6,4},{7,5},{8,10},{9,11},{10,... | collective-permute-start | bytes 1769480 | tf_op jit(solution)/shard_map/ppermute | solution.py:541
  184.3 17.4 %collective-permute-start.25 = (bf16[4,96,768]{2,1,0:T(8,128)(2,1)}, bf16[4,96,768]{2,1,0:T(8,128)(2,1)}, u32[]{:S(2)}, u32[]{:S(2)}) collective-permute-start(bf16[4,96,768]{2,1,0:T(8,128)(2,1)} %fusion.25), channel_id=1, source_target_pairs={{0,4},{4,0},{8,12},{12,8},{16,20},{20,16},{24,28},{28,24},{1,5},{5... | collective-permute-start | bytes 1769480 | tf_op jit(solution)/shard_map/ppermute | solution.py:541
  202.7 15.3 %collective-permute-start.27 = (bf16[4,96,768]{2,1,0:T(8,128)(2,1)}, bf16[4,96,768]{2,1,0:T(8,128)(2,1)}, u32[]{:S(2)}, u32[]{:S(2)}) collective-permute-start(bf16[4,96,768]{2,1,0:T(8,128)(2,1)} %fusion.27), channel_id=1, source_target_pairs={{0,4},{4,0},{8,12},{12,8},{16,20},{20,16},{24,28},{28,24},{1,5},{5... | collective-permute-start | bytes 1769480 | tf_op jit(solution)/shard_map/ppermute | solution.py:541
  206.2 14.8 %collective-permute-start.26 = (bf16[4,96,768]{2,1,0:T(8,128)(2,1)}, bf16[4,96,768]{2,1,0:T(8,128)(2,1)}, u32[]{:S(2)}, u32[]{:S(2)}) collective-permute-start(bf16[4,96,768]{2,1,0:T(8,128)(2,1)} %fusion.26), channel_id=1, source_target_pairs={{0,2},{1,3},{2,0},{3,1},{4,6},{5,7},{6,4},{7,5},{8,10},{9,11},{10,... | collective-permute-start | bytes 1769480 | tf_op jit(solution)/shard_map/ppermute | solution.py:541
  225.8 20.0 %collective-permute-start.33 = (bf16[4,96,768]{2,1,0:T(8,128)(2,1)}, bf16[4,96,768]{2,1,0:T(8,128)(2,1)}, u32[]{:S(2)}, u32[]{:S(2)}) collective-permute-start(bf16[4,96,768]{2,1,0:T(8,128)(2,1)} %fusion.22), channel_id=1, source_target_pairs={{0,4},{4,0},{8,12},{12,8},{16,20},{20,16},{24,28},{28,24},{1,5},{5... | collective-permute-start | bytes 1769480 | tf_op jit(solution)/shard_map/ppermute | solution.py:541
  226.6 19.2 %collective-permute-start.34 = (bf16[4,96,768]{2,1,0:T(8,128)(2,1)}, bf16[4,96,768]{2,1,0:T(8,128)(2,1)}, u32[]{:S(2)}, u32[]{:S(2)}) collective-permute-start(bf16[4,96,768]{2,1,0:T(8,128)(2,1)} %fusion.23), channel_id=1, source_target_pairs={{0,2},{1,3},{2,0},{3,1},{4,6},{5,7},{6,4},{7,5},{8,10},{9,11},{10,... | collective-permute-start | bytes 1769480 | tf_op jit(solution)/shard_map/ppermute | solution.py:541
  230.8 26.3 %collective-permute-start.29 = (bf16[768,384]{1,0:T(8,128)(2,1)}, bf16[768,384]{1,0:T(8,128)(2,1)}, u32[]{:S(2)}, u32[]{:S(2)}) collective-permute-start(bf16[768,384]{1,0:T(8,128)(2,1)} %fusion.28), channel_id=1, source_target_pairs={{0,2},{1,3},{2,0},{3,1},{4,6},{5,7},{6,4},{7,5},{8,10},{9,11},{10,... | collective-permute-start | bytes 1769480 | tf_op jit(solution)/shard_map/ppermute | solution.py:541
  232.3 24.8 %collective-permute-start.31 = (bf16[8,96,384]{2,1,0:T(8,128)(2,1)}, bf16[8,96,384]{2,1,0:T(8,128)(2,1)}, u32[]{:S(2)}, u32[]{:S(2)}) collective-permute-start(bf16[8,96,384]{2,1,0:T(8,128)(2,1)} %dynamic-slice_bitcast_fusion), channel_id=1, source_target_pairs={{0,4},{4,0},{8,12},{12,8},{16,20},{20,16},{24,28},{28,24},{1,5},{5... | collective-permute-start | bytes 1769480 | tf_op jit(solution)/shard_map/ppermute | solution.py:541
  246.8 10.4 %collective-permute-start.32 = (f32[22,768]{1,0:T(8,128)S(1)}, f32[22,768]{1,0:T(8,128)S(1)}, u32[]{:S(2)}, u32[]{:S(2)}) collective-permute-start(f32[22,768]{1,0:T(8,128)S(1)} %pad_maximum_fusion.5), channel_id=1, source_target_pairs={{0,1},{1,0},{2,3},{3,2},{4,5},{5,4},{6,7},{7,6},{8,9},{9,8},{10,11... | collective-permute-start | bytes 202760 | tf_op jit(solution)/shard_map/ppermute | solution.py:541
  251.3 17.4 %collective-permute-start.37 = (bf16[2,96,1536]{2,1,0:T(8,128)(2,1)}, bf16[2,96,1536]{2,1,0:T(8,128)(2,1)S(1)}, u32[]{:S(2)}, u32[]{:S(2)}) collective-permute-start(bf16[2,96,1536]{2,1,0:T(8,128)(2,1)} %fusion.32), channel_id=1, source_target_pairs={{0,8},{4,12},{8,0},{12,4},{16,24},{20,28},{24,16},{28,20},{1,9},{5... | collective-permute-start | bytes 1769480 | tf_op jit(solution)/shard_map/ppermute | solution.py:541
  259.3 10.7 %collective-permute-start.36 = (bf16[4,96,384]{2,1,0:T(8,128)(2,1)}, bf16[4,96,384]{2,1,0:T(8,128)(2,1)S(1)}, u32[]{:S(2)}, u32[]{:S(2)}) collective-permute-start(bf16[4,96,384]{2,1,0:T(8,128)(2,1)} %slice.179), channel_id=1, source_target_pairs={{0,2},{1,3},{2,0},{3,1},{4,6},{5,7},{6,4},{7,5},{8,10},{9,11},{10,... | collective-permute-start | bytes 884744 | tf_op jit(solution)/shard_map/ppermute | solution.py:541
  262.6 8.7 %collective-permute-start.35 = (bf16[4,96,384]{2,1,0:T(8,128)(2,1)}, bf16[4,96,384]{2,1,0:T(8,128)(2,1)S(1)}, u32[]{:S(2)}, u32[]{:S(2)}) collective-permute-start(bf16[4,96,384]{2,1,0:T(8,128)(2,1)} %dynamic-slice_bitcast_fusion.4), channel_id=1, source_target_pairs={{0,4},{4,0},{8,12},{12,8},{16,20},{20,16},{24,28},{28,24},{1,5},{5... | collective-permute-start | bytes 884744 | tf_op jit(solution)/shard_map/ppermute | solution.py:541
  273.2 15.8 %collective-permute-start.40 = (bf16[1,96,1536]{2,1,0:T(8,128)(2,1)S(1)}, bf16[1,96,1536]{2,1,0:T(8,128)(2,1)S(1)}, u32[]{:S(2)}, u32[]{:S(2)}) collective-permute-start(bf16[1,96,1536]{2,1,0:T(8,128)(2,1)S(1)} %constant_dynamic-slice_fusion.5), channel_id=1, source_target_pairs={{0,16},{4,20},{8,24},{12,28},{16,0},{20,4},{24,8},{28,12},{1,17},{... | collective-permute-start | bytes 884744 | tf_op jit(solution)/shard_map/ppermute | solution.py:541
  276.7 13.4 %collective-permute-start.39 = (bf16[2,96,768]{2,1,0:T(8,128)(2,1)S(1)}, bf16[2,96,768]{2,1,0:T(8,128)(2,1)S(1)}, u32[]{:S(2)}, u32[]{:S(2)}) collective-permute-start(bf16[2,96,768]{2,1,0:T(8,128)(2,1)S(1)} %fusion.36), channel_id=1, source_target_pairs={{0,8},{4,12},{8,0},{12,4},{16,24},{20,28},{24,16},{28,20},{1,9},{5... | collective-permute-start | bytes 884744 | tf_op jit(solution)/shard_map/ppermute | solution.py:541
  290.9 14.2 %collective-permute-start.42 = (bf16[1,96,768]{2,1,0:T(8,128)(2,1)S(1)}, bf16[1,96,768]{2,1,0:T(8,128)(2,1)S(1)}, u32[]{:S(2)}, u32[]{:S(2)}) collective-permute-start(bf16[1,96,768]{2,1,0:T(8,128)(2,1)S(1)} %constant_dynamic-slice_fusion.4), channel_id=1, source_target_pairs={{0,16},{4,20},{8,24},{12,28},{16,0},{20,4},{24,8},{28,12},{1,17},{... | collective-permute-start | bytes 442376 | tf_op jit(solution)/shard_map/ppermute | solution.py:541
  (63 other events, 298.2 us)

commit v2 on v1

--- a/solution.py
+++ b/solution.py
@@ -1030,9 +1030,7 @@
     ], axis=2))
     keep_m, send_m = halve_rows(mlp, data_bits[1])
     got_m = swap(send_m, "dp", data_bits[1])
-    owned = [own(v) for v in after((first_low, second_low, second_act, embed_grad), send_m)]
-    embed_low = after(embed_grad, send_m).astype(BF16)
-    got_a2, got_b2, small_got = after((got_a2, got_b2, small_got), embed_low, *owned)
+    got_a2, got_b2, small_got = after((got_a2, got_b2, small_got), send_m)
     keep_a, send_a = halve_rows(by_group(rounded(add(even_a[0], got_a[0]) + got_a2.astype(F32))), share)
     got_a = swap(send_a, "dp", share)
     sum_b = rounded(add(keep_b, got_b2)).reshape(2, groups // 2, width // groups, half)
@@ -1068,7 +1066,9 @@
     small = small + small_got
     small_got = swap(small, *small_bits[2])
 
-    own_first, own_second, own_act, own_embed = owned
+    first_low, second_low, second_act, embed_grad = after((first_low, second_low, second_act, embed_grad), send_m, send_j, small)
+    own_first, own_second, own_act, own_embed = [own(v) for v in (first_low, second_low, second_act, embed_grad)]
+    embed_low = embed_grad.astype(BF16)
     first_grad, second_grad, third_grad, first_bias_grad, second_bias_grad, third_bias_grad = call(
         head_grads_body,
         (

time: 313 us -> 313 us (level)
  waiting for transfers between devices: 46.3 us -> 41.4 us
    ppermute x45, waiting for transfers between devices: 46.3 us -> 41.4 us  [swap(): lax.ppermute(values, axis, [(i, i ^ bit) for i in range(lax.axis_size(axi...]
  transfers between devices with their start and end apart: 45 -> 45, of which waited for: 18 -> 17; matrix products, arithmetic and copies ran while one was open for 15% -> 15% of each run, Pallas kernels for 34% -> 34%
where the time goes in v2:
time: 313 us; the launch traced here: 307 us
  Pallas kernels  151 us (48%)
  waiting for transfers between devices  41.4 us (13%)
  starting transfers between devices  40.7 us (13%)
  other arithmetic  33.1 us (11%)
  local copies, waits for them, and re-layouts  32 us (10%)
  matrix products  6.32 us (2%)
    ppermute x45, waiting for transfers between devices, swap(): lax.ppermute(values, axis, [(i, i ^ bit) for i in range(lax.axis_size(axi...  41.4 us
    ppermute x45, starting transfers between devices, swap(): lax.ppermute(values, axis, [(i, i ^ bit) for i in range(lax.axis_size(axi...  40.7 us
    pallas_call x2, Pallas kernels, inner_back(): pl.pallas_call(functools.partial(inner_back_body, windows, pieces, bool(b...  34.8 us
    pallas_call x3, Pallas kernels, inner_call(): pl.pallas_call(functools.partial(inner_body, n, pieces, bool(before), las...  31.7 us
    pallas_call x5, Pallas kernels, call(): pl.pallas_call(body, out_shape=outs, in_specs=[pl.BlockSpec(memory_space=...  27.6 us
    pallas_call x2, Pallas kernels, attend(): pl.pallas_call(functools.partial(attend_body, size, scale), grid=(padded_...  17.2 us
    convert_element_type x10, other arithmetic, rounded(): return value.astype(BF16)  16.9 us
    pallas_call x1, Pallas kernels, shards(): pl.pallas_call(functools.partial(attend_back_body, size, scale), grid=(pa...  12.4 us
  transfers between devices with their start and end apart: 45, of which 17 were waited for; matrix products, arithmetic and copies ran while one was open for 15% of the time, Pallas kernels for 34%

profile of v2, /device:TPU:0, one launch (start us, length us, event | category | flops | bytes accessed | tf_op | source)
XLA Modules:
  0.0 306.7 jit_solution(15289113443483051701)
XLA Ops:
  1.7 3.0 collective-permute-start
  7.2 3.2 %fusion.12 = f32[64,24,64]{2,1,0:T(8,128)S(1)} fusion(f32[24,169,1]{1,0,2:T(8,128)S(1)} %reshape.448, s32[64,64]{1,0:T(8,128)S(1)} %add_select_fusion, pred[64]{0:T(512)(128)(4,1)S(1)} %iota_compare_fusion.3), kind=kOutput, calls=%fused_computation.18 | convolution fusion | flops 200151040 | bytes 425888 | tf_op jit(solution)/shard_map/dot_general | solution.py:680
  11.4 3.6 %shard_map.365.padded.x = bf16[1024,768]{1,0:T(8,128)(2,1)} custom-call(bf16[784,768]{1,0:T(8,128)(2,1)} %tokens.3, f32[3,768]{1,0:T(4,128)} %gains.5, f32[5,768]{1,0:T(8,128)} %refs_9_.2), custom_call_target="tpu_custom_call" | custom-call | bytes 11550000 | tf_op jit(solution)/shard_map/pallas_call | solution.py:40
  18.9 8.5 %shard_map.366 = (bf16[1024,1152]{1,0:T(8,128)(2,1)}, bf16[1024,768]{1,0:T(8,128)(2,1)}, bf16[1024,384]{1,0:T(8,128)(2,1)}, bf16[3,384,768]{2,1,0:T(8,128)(2,1)}) custom-call(bf16[1024,768]{1,0:T(8,128)(2,1)} %shard_map.365.padded.x, bf16[3,192,768]{2,1,0:T(8,128)(2,1)} %bitcast.215, bf16[3,192,768]{2,1,0:T(8,128)(2,1)} %copy-done.25, ...), custom_call_target="tpu_custom_call" | custom-call | bytes 29700000 | tf_op jit(solution)/shard_map/pallas_call | solution.py:705
  31.5 8.7 %shard_map.367 = (bf16[1024,1152]{1,0:T(8,128)(2,1)}, bf16[1024,768]{1,0:T(8,128)(2,1)}, bf16[1024,384]{1,0:T(8,128)(2,1)}, bf16[3,384,768]{2,1,0:T(8,128)(2,1)}) custom-call(bf16[1024,768]{1,0:T(8,128)(2,1)} %shard_map.365.padded.x, bf16[3,192,768]{2,1,0:T(8,128)(2,1)} %bitcast.205, bf16[3,192,768]{2,1,0:T(8,128)(2,1)} %collective-permute-done.4.far, ...), custom_call_target="tpu_custom_call" | custom-call | bytes 29700000 | tf_op jit(solution)/shard_map/pallas_call | solution.py:705
  40.2 5.1 %collective-permute-done.7 = bf16[384,768]{1,0:T(8,128)(2,1)} collective-permute-done((bf16[384,768]{1,0:T(8,128)(2,1)}, bf16[384,768]{1,0:T(8,128)(2,1)}, u32[]{:S(2)}, u32[]{:S(2)}) %collective-permute-start.7) | collective-permute-done | bytes 589856 | tf_op jit(solution)/shard_map/ppermute | solution.py:541
  49.1 6.3 %shard_map.368 = (f32[784,768]{1,0:T(8,128)}, bf16[784,768]{1,0:T(8,128)(2,1)}, bf16[768,768]{1,0:T(8,128)(2,1)}) custom-call(bf16[1024,384]{1,0:T(8,128)(2,1)} %get-tuple-element.151.att0, bf16[1024,384]{1,0:T(8,128)(2,1)} %get-tuple-element.158.att1, bf16[192,768]{1,0:T(8,128)(2,1)} %refs_0_.1, bf16[192,768]{1,0:T(8,128)(2,1)} %collective-permute-done.5.refs_1_, ...), custom_call_target="tpu_custom_call" | custom-call | bytes 19800000 | tf_op jit(solution)/shard_map/pallas_call | solution.py:40
  55.4 7.7 %shard_map.369 = (bf16[784,768]{1,0:T(8,128)(2,1)}, bf16[784,768]{1,0:T(8,128)(2,1)}, f32[784,768]{1,0:T(8,128)}) custom-call(bf16[784,768]{1,0:T(8,128)(2,1)} %get-tuple-element.172.refs_0_.refs_1_, f32[1,1,768]{2,1,0:T(1,128)} %get-tuple-element.377.refs_1_, bf16[768,768]{1,0:T(8,128)(2,1)} %refs_7_.1, bf16[768,768]{1,0:T(8,128)(2,1)} %refs_9_.3), custom_call_target="tpu_custom_call" | custom-call | bytes 23100000 | tf_op jit(solution)/shard_map/pallas_call | solution.py:775
  66.3 7.8 %shard_map.370 = (bf16[784,768]{1,0:T(8,128)(2,1)}, bf16[784,768]{1,0:T(8,128)(2,1)}, f32[784,768]{1,0:T(8,128)}) custom-call(bf16[784,768]{1,0:T(8,128)(2,1)} %get-tuple-element.172.refs_0_.refs_1_, f32[1,1,768]{2,1,0:T(1,128)} %get-tuple-element.376.refs_1_, bf16[768,768]{1,0:T(8,128)(2,1)} %collective-permute-done.12.refs_2_.refs_7_, ...), custom_call_target="tpu_custom_call" | custom-call | bytes 23100000 | tf_op jit(solution)/shard_map/pallas_call | solution.py:775
  76.3 4.4 %collective-permute-done.11 = bf16[384,768]{1,0:T(8,128)(2,1)} collective-permute-done((bf16[384,768]{1,0:T(8,128)(2,1)}, bf16[384,768]{1,0:T(8,128)(2,1)}, u32[]{:S(2)}, u32[]{:S(2)}) %collective-permute-start.11) | collective-permute-done | bytes 589856 | tf_op jit(solution)/shard_map/ppermute | solution.py:541
  86.0 16.2 %shard_map.371 = (bf16[784,768]{1,0:T(8,128)(2,1)}, bf16[784,768]{1,0:T(8,128)(2,1)}, bf16[784,768]{1,0:T(8,128)(2,1)}, bf16[784,768]{1,0:T(8,128)(2,1)}, f32[78...) custom-call(bf16[784,768]{1,0:T(8,128)(2,1)} %get-tuple-element.172.refs_0_.refs_1_, ...), custom_call_target="tpu_custom_call" | custom-call | bytes 52800000 | tf_op jit(solution)/shard_map/pallas_call | solution.py:775
  109.4 3.2 %collective-permute-done.17 = f32[88,128]{1,0:T(8,128)S(1)} collective-permute-done((f32[88,128]{1,0:T(8,128)S(1)}, f32[88,128]{1,0:T(8,128)S(1)}, u32[]{:S(2)}, u32[]{:S(2)}) %collective-permute-start.17) | collective-permute-done | bytes 45088 | tf_op jit(solution)/shard_map/ppermute | solution.py:541
  114.3 2.6 collective-permute-done.18
  116.9 3.3 %collective-permute-start.19 = (f32[160,128]{1,0:T(8,128)S(1)}, f32[160,128]{1,0:T(8,128)S(1)}, u32[]{:S(2)}, u32[]{:S(2)}) collective-permute-start(f32[160,128]{1,0:T(8,128)S(1)} %pad_maximum_fusion.4), channel_id=1, source_target_pairs={{0,16},{4,20},{8,24},{12,28},{16,0},{20,4},{24,8},{28,12},{1,17},{... | collective-permute-start | bytes 245768 | tf_op jit(solution)/shard_map/ppermute | solution.py:541
  120.2 3.3 %collective-permute-done.19 = f32[160,128]{1,0:T(8,128)S(1)} collective-permute-done((f32[160,128]{1,0:T(8,128)S(1)}, f32[160,128]{1,0:T(8,128)S(1)}, u32[]{:S(2)}, u32[]{:S(2)}) %collective-permute-start.19) | collective-permute-done | bytes 81952 | tf_op jit(solution)/shard_map/ppermute | solution.py:541
  124.8 10.7 %shard_map.372 = (bf16[32,2048]{1,0:T(8,128)(2,1)}, bf16[32,2048]{1,0:T(8,128)(2,1)}, bf16[32,256]{1,0:T(8,128)(2,1)}, f32[32,256]{1,0:T(8,128)}, bf16[32,2048]{...) custom-call(bf16[32,768]{1,0:T(8,128)(2,1)} %convert_element_type.252.pooled, ...), custom_call_target="tpu_custom_call" | custom-call | bytes 29700000 | tf_op jit(solution)/shard_map/pallas_call | solution.py:830
  136.9 5.4 %shard_map.373 = (f32[784,768]{1,0:T(8,128)}, bf16[784,768]{1,0:T(8,128)(2,1)}, f32[3,768]{1,0:T(4,128)}) custom-call(f32[784,768]{1,0:T(8,128)} %get-tuple-element.181.block_out, bf16[784,768]{1,0:T(8,128)(2,1)} %cotangent.2, s32[784,1]{1,0:T(8,128)} %broadcast_in_dim.65.refs_10_.crop, f32[4,768]{1,0:T(4,128)} %dynamic-slice_divide_fusion.pooled_grad, ...), custom_call_target="tpu_custom_call" | custom-call | bytes 13200000 | tf_op jit(solution)/shard_map/pallas_call | solution.py:863
  142.3 15.7 %shard_map.374 = (bf16[768,768]{1,0:T(8,128)(2,1)}, bf16[768,768]{1,0:T(8,128)(2,1)}, bf16[768,768]{1,0:T(8,128)(2,1)}, bf16[768,768]{1,0:T(8,128)(2,1)}, f32[2,768]{1,0:T(2,128)}, /*index=5*/f32[784,768]{1,0:T(8,128)}) custom-call(bf16[784,768]{1,0:T(8,128)(2,1)} %get-tuple-element.183.refs_0_, bf16[784,768]{1,0:T(8,128)(2,1)} %get-tuple-element.172.refs_0_.refs_1_, ...), custom_call_target="tpu_custom_call" | custom-call | bytes 49500000 | tf_op jit(solution)/shard_map/pallas_call | solution.py:886
  159.1 19.1 %shard_map.375 = (bf16[768,768]{1,0:T(8,128)(2,1)}, bf16[768,768]{1,0:T(8,128)(2,1)}, bf16[768,768]{1,0:T(8,128)(2,1)}, bf16[768,768]{1,0:T(8,128)(2,1)}, f32[2,...) custom-call(bf16[784,768]{1,0:T(8,128)(2,1)} %get-tuple-element.183.refs_0_, ...), custom_call_target="tpu_custom_call" | custom-call | bytes 59400000 | tf_op jit(solution)/shard_map/pallas_call | solution.py:886
  178.3 3.4 %fusion.24 = bf16[4,96,768]{2,1,0:T(8,128)(2,1)} fusion(bf16[4,2,96,768]{3,2,1,0:T(8,128)(2,1)} %bitcast.27, s32[]{:T(128)S(6)} %select_n.489, bf16[4,2,96,768]{3,2,1,0:T(8,128)(2,1)} %bitcast.230), kind=kLoop, calls=%fused_computation.49 | loop fusion | flops 1179648 | bytes 1769476 | tf_op jit(solution)/shard_map/convert_element_type | solution.py:927
  185.7 12.4 %shard_map.376 = (bf16[1024,2304]{1,0:T(8,128)(2,1)}, f32[64,1536]{1,0:T(8,128)}, f32[1,2304]{1,0:T(1,128)}) custom-call(bf16[1024,768]{1,0:T(8,128)(2,1)} %get-tuple-element.203.low, bf16[768,768]{1,0:T(8,128)(2,1)} %get-tuple-element.204.weight, bf16[1024,1152]{1,0:T(8,128)(2,1)} %get-tuple-element.152.qkv0, bf16[1024,1152]{1,0:T(8,128)(2,1)} %get-tuple-element.161.qkv1, ...), custom_call_target="tpu_custom_call" | custom-call | bytes 42900000 | tf_op jit(solution)/shard_map/pallas_call | solution.py:935
  206.7 11.5 %shard_map.377 = (bf16[2,768,384]{2,1,0:T(8,128)(2,1)}, bf16[2,768,384]{2,1,0:T(8,128)(2,1)}, bf16[2,768,384]{2,1,0:T(8,128)(2,1)}, bf16[2,768,384]{2,1,0:T(8,128)(2,1)}) custom-call(bf16[1024,768]{1,0:T(8,128)(2,1)} %shard_map.365.padded.x, bf16[1024,768]{1,0:T(8,128)(2,1)} %get-tuple-element.203.low, bf16[1024,2304]{1,0:T(8,128)(2,1)} %get-tuple-element.226.d.grads, ...), custom_call_target="tpu_custom_call" | custom-call | bytes 39600000 | tf_op jit(solution)/shard_map/pallas_call | solution.py:970
  218.2 3.0 collective-permute-done.26
  228.6 2.4 fusion.28
  235.2 10.8 %shard_map.378 = (f32[784,768]{1,0:T(8,128)}, f32[14,768]{1,0:T(8,128)}) custom-call(bf16[1024,2304]{1,0:T(8,128)(2,1)} %get-tuple-element.226.d.grads, bf16[1152,768]{1,0:T(8,128)(2,1)} %bitcast.216, bf16[1152,768]{1,0:T(8,128)(2,1)} %bitcast.217, bf16[784,768]{1,0:T(8,128)(2,1)} %tokens.3, f32[784,768]{1,0:T(8,128)} %get-tuple-element.227.mixed_grad, ...), custom_call_target="tpu_custom_call" | custom-call | bytes 33000000 | tf_op jit(solution)/shard_map/pallas_call | solution.py:40
  252.1 2.6 collective-permute-done.29
  262.7 4.0 %shard_map.379 = (f32[32,2048]{1,0:T(8,128)}, f32[256,2048]{1,0:T(8,128)}, f32[1,2048]{1,0:T(1,128)}) custom-call(bf16[32,256]{1,0:T(8,128)(2,1)} %get-tuple-element.245.units, bf16[256,2048]{1,0:T(8,128)(2,1)} %copy-done.3, bf16[32,2048]{1,0:T(8,128)(2,1)} %cotangent.3, bf16[256,2048]{1,0:T(8,128)(2,1)} %direction.1, f32[1,2048]{1,0:T(1,128)} %bitcast.233, ...), custom_call_target="tpu_custom_call" | custom-call | bytes 13200000 | tf_op jit(solution)/shard_map/pallas_call | solution.py:40
  271.6 2.7 collective-permute-start.40
  280.9 3.0 shard_map.380
  283.9 3.2 %collective-permute-done.40 = bf16[1,96,1536]{2,1,0:T(8,128)(2,1)S(1)} collective-permute-done((bf16[1,96,1536]{2,1,0:T(8,128)(2,1)S(1)}, bf16[1,96,1536]{2,1,0:T(8,128)(2,1)S(1)}, u32[]{:S(2)}, u32[]{:S(2)}) %collective-permute-start.40) | collective-permute-done | bytes 294944 | tf_op jit(solution)/shard_map/ppermute | solution.py:541
  289.4 2.4 collective-permute-start.42
  295.7 6.1 %collective-permute-done.44 = f32[22,768]{1,0:T(8,128)S(1)} collective-permute-done((f32[22,768]{1,0:T(8,128)S(1)}, f32[22,768]{1,0:T(8,128)S(1)}, u32[]{:S(2)}, u32[]{:S(2)}) %collective-permute-start.44) | collective-permute-done | bytes 67616 | tf_op jit(solution)/shard_map/ppermute | solution.py:541
  (312 shorter events, 99.7 us)
Async XLA Ops:
  1.7 13.2 %collective-permute-start = (bf16[288,768]{1,0:T(8,128)(2,1)S(1)}, bf16[288,768]{1,0:T(8,128)(2,1)S(1)}, u32[]{:S(2)}, u32[]{:S(2)}) collective-permute-start(bf16[288,768]{1,0:T(8,128)(2,1)S(1)} %dynamic-slice_bitcast_fusion.3), channel_id=1, source_target_pairs={{0,2},{1,3},{2,0},{3,1},{4,6},{5,7},{6,4},{7,5},{8,10},{9,11},{10,... | collective-permute-start | bytes 1327112 | tf_op jit(solution)/shard_map/ppermute | solution.py:541
  4.7 10.2 %collective-permute-start.1 = (bf16[3,192,768]{2,1,0:T(8,128)(2,1)}, bf16[3,192,768]{2,1,0:T(8,128)(2,1)S(1)}, u32[]{:S(2)}, u32[]{:S(2)}) collective-permute-start(bf16[3,192,768]{2,1,0:T(8,128)(2,1)} %bitcast.214), channel_id=1, source_target_pairs={{0,1},{1,0},{2,3},{3,2},{4,5},{5,4},{6,7},{7,6},{8,9},{9,8},{10,11... | collective-permute-start | bytes 2654216 | tf_op jit(solution)/shard_map/ppermute | solution.py:541
  14.9 12.6 %collective-permute-start.2 = (bf16[288,768]{1,0:T(8,128)(2,1)S(1)}, bf16[288,768]{1,0:T(8,128)(2,1)S(1)}, u32[]{:S(2)}, u32[]{:S(2)}) collective-permute-start(bf16[288,768]{1,0:T(8,128)(2,1)S(1)} %collective-permute-done), channel_id=1, source_target_pairs={{0,4},{4,0},{8,12},{12,8},{16,20},{20,16},{24,28},{28,24},{1,5},{5... | collective-permute-start | bytes 1327112 | tf_op jit(solution)/shard_map/ppermute | solution.py:541
  16.7 10.7 %collective-permute-start.3 = (bf16[192,768]{1,0:T(8,128)(2,1)}, bf16[192,768]{1,0:T(8,128)(2,1)S(1)}, u32[]{:S(2)}, u32[]{:S(2)}) collective-permute-start(bf16[192,768]{1,0:T(8,128)(2,1)} %refs_0_.1), channel_id=1, source_target_pairs={{0,2},{1,3},{2,0},{3,1},{4,6},{5,7},{6,4},{7,5},{8,10},{9,11},{10,... | collective-permute-start | bytes 884744 | tf_op jit(solution)/shard_map/ppermute | solution.py:541
  30.1 15.3 %collective-permute-start.7 = (bf16[384,768]{1,0:T(8,128)(2,1)}, bf16[384,768]{1,0:T(8,128)(2,1)}, u32[]{:S(2)}, u32[]{:S(2)}) collective-permute-start(bf16[384,768]{1,0:T(8,128)(2,1)} %dynamic-slice_bitcast_fusion.2), channel_id=1, source_target_pairs={{0,2},{1,3},{2,0},{3,1},{4,6},{5,7},{6,4},{7,5},{8,10},{9,11},{10,... | collective-permute-start | bytes 1769480 | tf_op jit(solution)/shard_map/ppermute | solution.py:541
  30.5 9.7 %collective-permute-start.6 = (bf16[192,768]{1,0:T(8,128)(2,1)S(1)}, bf16[192,768]{1,0:T(8,128)(2,1)}, u32[]{:S(2)}, u32[]{:S(2)}) collective-permute-start(bf16[192,768]{1,0:T(8,128)(2,1)S(1)} %collective-permute-done.3.refs_2_), channel_id=1, source_target_pairs={{0,1},{1,0},{2,3},{3,2},{4,5},{5,4},{6,7},{7,6},{8,9},{9,8},{10,11... | collective-permute-start | bytes 884744 | tf_op jit(solution)/shard_map/ppermute | solution.py:541
  30.5 18.6 %collective-permute-start.5 = (bf16[192,768]{1,0:T(8,128)(2,1)}, bf16[192,768]{1,0:T(8,128)(2,1)}, u32[]{:S(2)}, u32[]{:S(2)}) collective-permute-start(bf16[192,768]{1,0:T(8,128)(2,1)} %refs_0_.1), channel_id=1, source_target_pairs={{0,1},{1,0},{2,3},{3,2},{4,5},{5,4},{6,7},{7,6},{8,9},{9,8},{10,11... | collective-permute-start | bytes 884744 | tf_op jit(solution)/shard_map/ppermute | solution.py:541
  31.0 35.3 %collective-permute-start.12 = (bf16[768,768]{1,0:T(8,128)(2,1)S(1)}, bf16[768,768]{1,0:T(8,128)(2,1)}, u32[]{:S(2)}, u32[]{:S(2)}) collective-permute-start(bf16[768,768]{1,0:T(8,128)(2,1)S(1)} %copy-done.4), channel_id=1, source_target_pairs={{0,1},{1,0},{2,3},{3,2},{4,5},{5,4},{6,7},{7,6},{8,9},{9,8},{10,11... | collective-permute-start | bytes 3538952 | tf_op jit(solution)/shard_map/ppermute | solution.py:541
  31.0 35.3 %collective-permute-start.13 = (bf16[768,768]{1,0:T(8,128)(2,1)S(1)}, bf16[768,768]{1,0:T(8,128)(2,1)}, u32[]{:S(2)}, u32[]{:S(2)}) collective-permute-start(bf16[768,768]{1,0:T(8,128)(2,1)S(1)} %copy-done.5), channel_id=1, source_target_pairs={{0,1},{1,0},{2,3},{3,2},{4,5},{5,4},{6,7},{7,6},{8,9},{9,8},{10,11... | collective-permute-start | bytes 3538952 | tf_op jit(solution)/shard_map/ppermute | solution.py:541
  45.4 17.7 %collective-permute-start.9 = (bf16[384,768]{1,0:T(8,128)(2,1)}, bf16[384,768]{1,0:T(8,128)(2,1)S(1)}, u32[]{:S(2)}, u32[]{:S(2)}) collective-permute-start(bf16[384,768]{1,0:T(8,128)(2,1)} %collective-permute-done.7), channel_id=1, source_target_pairs={{0,4},{4,0},{8,12},{12,8},{16,20},{20,16},{24,28},{28,24},{1,5},{5... | collective-permute-start | bytes 1769480 | tf_op jit(solution)/shard_map/ppermute | solution.py:541
  47.6 15.5 %collective-permute-start.8 = (bf16[384,768]{1,0:T(8,128)(2,1)}, bf16[384,768]{1,0:T(8,128)(2,1)S(1)}, u32[]{:S(2)}, u32[]{:S(2)}) collective-permute-start(bf16[384,768]{1,0:T(8,128)(2,1)} %dynamic-slice_bitcast_fusion.1), channel_id=1, source_target_pairs={{0,2},{1,3},{2,0},{3,1},{4,6},{5,7},{6,4},{7,5},{8,10},{9,11},{10,... | collective-permute-start | bytes 1769480 | tf_op jit(solution)/shard_map/ppermute | solution.py:541
  64.6 16.1 %collective-permute-start.10 = (bf16[768,768]{1,0:T(8,128)(2,1)S(1)}, bf16[768,768]{1,0:T(8,128)(2,1)}, u32[]{:S(2)}, u32[]{:S(2)}) collective-permute-start(bf16[768,768]{1,0:T(8,128)(2,1)S(1)} %pad_maximum_fusion.refs_2_.refs_6_), channel_id=1, source_target_pairs={{0,1},{1,0},{2,3},{3,2},{4,5},{5,4},{6,7},{7,6},{8,9},{9,8},{10,11... | collective-permute-start | bytes 3538952 | tf_op jit(solution)/shard_map/ppermute | solution.py:541
  64.7 16.1 %collective-permute-start.11 = (bf16[384,768]{1,0:T(8,128)(2,1)}, bf16[384,768]{1,0:T(8,128)(2,1)}, u32[]{:S(2)}, u32[]{:S(2)}) collective-permute-start(bf16[384,768]{1,0:T(8,128)(2,1)} %copy-done.26), channel_id=1, source_target_pairs={{0,8},{4,12},{8,0},{12,4},{16,24},{20,28},{24,16},{28,20},{1,9},{5... | collective-permute-start | bytes 1769480 | tf_op jit(solution)/shard_map/ppermute | solution.py:541
  158.0 20.2 %collective-permute-start.20 = (bf16[768,768]{1,0:T(8,128)(2,1)}, bf16[768,768]{1,0:T(8,128)(2,1)S(1)}, u32[]{:S(2)}, u32[]{:S(2)}) collective-permute-start(bf16[768,768]{1,0:T(8,128)(2,1)} %get-tuple-element.196), channel_id=1, source_target_pairs={{0,1},{1,0},{2,3},{3,2},{4,5},{5,4},{6,7},{7,6},{8,9},{9,8},{10,11... | collective-permute-start | bytes 3538952 | tf_op jit(solution)/shard_map/ppermute | solution.py:541
  158.1 20.1 %collective-permute-start.21 = (bf16[768,768]{1,0:T(8,128)(2,1)}, bf16[768,768]{1,0:T(8,128)(2,1)}, u32[]{:S(2)}, u32[]{:S(2)}) collective-permute-start(bf16[768,768]{1,0:T(8,128)(2,1)} %get-tuple-element.197), channel_id=1, source_target_pairs={{0,1},{1,0},{2,3},{3,2},{4,5},{5,4},{6,7},{7,6},{8,9},{9,8},{10,11... | collective-permute-start | bytes 3538952 | tf_op jit(solution)/shard_map/ppermute | solution.py:541
  158.6 19.7 %collective-permute-start.22 = (bf16[768,768]{1,0:T(8,128)(2,1)}, bf16[768,768]{1,0:T(8,128)(2,1)S(1)}, u32[]{:S(2)}, u32[]{:S(2)}) collective-permute-start(bf16[768,768]{1,0:T(8,128)(2,1)} %get-tuple-element.198), channel_id=1, source_target_pairs={{0,1},{1,0},{2,3},{3,2},{4,5},{5,4},{6,7},{7,6},{8,9},{9,8},{10,11... | collective-permute-start | bytes 3538952 | tf_op jit(solution)/shard_map/ppermute | solution.py:541
  158.7 19.6 %collective-permute-start.23 = (bf16[768,768]{1,0:T(8,128)(2,1)}, bf16[768,768]{1,0:T(8,128)(2,1)S(1)}, u32[]{:S(2)}, u32[]{:S(2)}) collective-permute-start(bf16[768,768]{1,0:T(8,128)(2,1)} %get-tuple-element.199), channel_id=1, source_target_pairs={{0,1},{1,0},{2,3},{3,2},{4,5},{5,4},{6,7},{7,6},{8,9},{9,8},{10,11... | collective-permute-start | bytes 3538952 | tf_op jit(solution)/shard_map/ppermute | solution.py:541
  181.7 20.1 %collective-permute-start.24 = (bf16[4,96,768]{2,1,0:T(8,128)(2,1)}, bf16[4,96,768]{2,1,0:T(8,128)(2,1)}, u32[]{:S(2)}, u32[]{:S(2)}) collective-permute-start(bf16[4,96,768]{2,1,0:T(8,128)(2,1)} %fusion.24), channel_id=1, source_target_pairs={{0,2},{1,3},{2,0},{3,1},{4,6},{5,7},{6,4},{7,5},{8,10},{9,11},{10,... | collective-permute-start | bytes 1769480 | tf_op jit(solution)/shard_map/ppermute | solution.py:541
  184.4 17.4 %collective-permute-start.25 = (bf16[4,96,768]{2,1,0:T(8,128)(2,1)}, bf16[4,96,768]{2,1,0:T(8,128)(2,1)}, u32[]{:S(2)}, u32[]{:S(2)}) collective-permute-start(bf16[4,96,768]{2,1,0:T(8,128)(2,1)} %fusion.25), channel_id=1, source_target_pairs={{0,4},{4,0},{8,12},{12,8},{16,20},{20,16},{24,28},{28,24},{1,5},{5... | collective-permute-start | bytes 1769480 | tf_op jit(solution)/shard_map/ppermute | solution.py:541
  202.8 15.3 %collective-permute-start.27 = (bf16[4,96,768]{2,1,0:T(8,128)(2,1)}, bf16[4,96,768]{2,1,0:T(8,128)(2,1)}, u32[]{:S(2)}, u32[]{:S(2)}) collective-permute-start(bf16[4,96,768]{2,1,0:T(8,128)(2,1)} %fusion.27), channel_id=1, source_target_pairs={{0,4},{4,0},{8,12},{12,8},{16,20},{20,16},{24,28},{28,24},{1,5},{5... | collective-permute-start | bytes 1769480 | tf_op jit(solution)/shard_map/ppermute | solution.py:541
  206.4 14.8 %collective-permute-start.26 = (bf16[4,96,768]{2,1,0:T(8,128)(2,1)}, bf16[4,96,768]{2,1,0:T(8,128)(2,1)}, u32[]{:S(2)}, u32[]{:S(2)}) collective-permute-start(bf16[4,96,768]{2,1,0:T(8,128)(2,1)} %fusion.26), channel_id=1, source_target_pairs={{0,2},{1,3},{2,0},{3,1},{4,6},{5,7},{6,4},{7,5},{8,10},{9,11},{10,... | collective-permute-start | bytes 1769480 | tf_op jit(solution)/shard_map/ppermute | solution.py:541
  226.1 20.0 %collective-permute-start.33 = (bf16[4,96,768]{2,1,0:T(8,128)(2,1)}, bf16[4,96,768]{2,1,0:T(8,128)(2,1)}, u32[]{:S(2)}, u32[]{:S(2)}) collective-permute-start(bf16[4,96,768]{2,1,0:T(8,128)(2,1)} %fusion.22), channel_id=1, source_target_pairs={{0,4},{4,0},{8,12},{12,8},{16,20},{20,16},{24,28},{28,24},{1,5},{5... | collective-permute-start | bytes 1769480 | tf_op jit(solution)/shard_map/ppermute | solution.py:541
  226.8 19.2 %collective-permute-start.34 = (bf16[4,96,768]{2,1,0:T(8,128)(2,1)}, bf16[4,96,768]{2,1,0:T(8,128)(2,1)}, u32[]{:S(2)}, u32[]{:S(2)}) collective-permute-start(bf16[4,96,768]{2,1,0:T(8,128)(2,1)} %fusion.23), channel_id=1, source_target_pairs={{0,2},{1,3},{2,0},{3,1},{4,6},{5,7},{6,4},{7,5},{8,10},{9,11},{10,... | collective-permute-start | bytes 1769480 | tf_op jit(solution)/shard_map/ppermute | solution.py:541
  231.0 23.7 %collective-permute-start.29 = (bf16[768,384]{1,0:T(8,128)(2,1)}, bf16[768,384]{1,0:T(8,128)(2,1)}, u32[]{:S(2)}, u32[]{:S(2)}) collective-permute-start(bf16[768,384]{1,0:T(8,128)(2,1)} %fusion.28), channel_id=1, source_target_pairs={{0,2},{1,3},{2,0},{3,1},{4,6},{5,7},{6,4},{7,5},{8,10},{9,11},{10,... | collective-permute-start | bytes 1769480 | tf_op jit(solution)/shard_map/ppermute | solution.py:541
  232.6 22.1 %collective-permute-start.31 = (bf16[8,96,384]{2,1,0:T(8,128)(2,1)}, bf16[8,96,384]{2,1,0:T(8,128)(2,1)}, u32[]{:S(2)}, u32[]{:S(2)}) collective-permute-start(bf16[8,96,384]{2,1,0:T(8,128)(2,1)} %dynamic-slice_bitcast_fusion), channel_id=1, source_target_pairs={{0,4},{4,0},{8,12},{12,8},{16,20},{20,16},{24,28},{28,24},{1,5},{5... | collective-permute-start | bytes 1769480 | tf_op jit(solution)/shard_map/ppermute | solution.py:541
  251.6 15.6 %collective-permute-start.37 = (bf16[2,96,1536]{2,1,0:T(8,128)(2,1)}, bf16[2,96,1536]{2,1,0:T(8,128)(2,1)S(1)}, u32[]{:S(2)}, u32[]{:S(2)}) collective-permute-start(bf16[2,96,1536]{2,1,0:T(8,128)(2,1)} %fusion.32), channel_id=1, source_target_pairs={{0,8},{4,12},{8,0},{12,4},{16,24},{20,28},{24,16},{28,20},{1,9},{5... | collective-permute-start | bytes 1769480 | tf_op jit(solution)/shard_map/ppermute | solution.py:541
  256.7 10.5 %collective-permute-start.36 = (bf16[4,96,384]{2,1,0:T(8,128)(2,1)}, bf16[4,96,384]{2,1,0:T(8,128)(2,1)S(1)}, u32[]{:S(2)}, u32[]{:S(2)}) collective-permute-start(bf16[4,96,384]{2,1,0:T(8,128)(2,1)} %slice.179), channel_id=1, source_target_pairs={{0,2},{1,3},{2,0},{3,1},{4,6},{5,7},{6,4},{7,5},{8,10},{9,11},{10,... | collective-permute-start | bytes 884744 | tf_op jit(solution)/shard_map/ppermute | solution.py:541
  270.7 13.2 %collective-permute-start.41 = (f32[22,768]{1,0:T(8,128)}, f32[22,768]{1,0:T(8,128)S(1)}, u32[]{:S(2)}, u32[]{:S(2)}) collective-permute-start(f32[22,768]{1,0:T(8,128)} %add.397), channel_id=1, source_target_pairs={{0,4},{4,0},{8,12},{12,8},{16,20},{20,16},{24,28},{28,24},{1,5},{5... | collective-permute-start | bytes 202760 | tf_op jit(solution)/shard_map/ppermute | solution.py:541
  271.6 15.5 %collective-permute-start.40 = (bf16[1,96,1536]{2,1,0:T(8,128)(2,1)S(1)}, bf16[1,96,1536]{2,1,0:T(8,128)(2,1)S(1)}, u32[]{:S(2)}, u32[]{:S(2)}) collective-permute-start(bf16[1,96,1536]{2,1,0:T(8,128)(2,1)S(1)} %constant_dynamic-slice_fusion.1), channel_id=1, source_target_pairs={{0,16},{4,20},{8,24},{12,28},{16,0},{20,4},{24,8},{28,12},{1,17},{... | collective-permute-start | bytes 884744 | tf_op jit(solution)/shard_map/ppermute | solution.py:541
  274.4 12.9 %collective-permute-start.39 = (bf16[2,96,768]{2,1,0:T(8,128)(2,1)S(1)}, bf16[2,96,768]{2,1,0:T(8,128)(2,1)S(1)}, u32[]{:S(2)}, u32[]{:S(2)}) collective-permute-start(bf16[2,96,768]{2,1,0:T(8,128)(2,1)S(1)} %fusion.36), channel_id=1, source_target_pairs={{0,8},{4,12},{8,0},{12,4},{16,24},{20,28},{24,16},{28,20},{1,9},{5... | collective-permute-start | bytes 884744 | tf_op jit(solution)/shard_map/ppermute | solution.py:541
  289.4 15.5 %collective-permute-start.42 = (bf16[1,96,768]{2,1,0:T(8,128)(2,1)S(1)}, bf16[1,96,768]{2,1,0:T(8,128)(2,1)S(1)}, u32[]{:S(2)}, u32[]{:S(2)}) collective-permute-start(bf16[1,96,768]{2,1,0:T(8,128)(2,1)S(1)} %constant_dynamic-slice_fusion.4), channel_id=1, source_target_pairs={{0,16},{4,20},{8,24},{12,28},{16,0},{20,4},{24,8},{28,12},{1,17},{... | collective-permute-start | bytes 442376 | tf_op jit(solution)/shard_map/ppermute | solution.py:541
  293.6 8.2 %collective-permute-start.44 = (f32[22,768]{1,0:T(8,128)S(1)}, f32[22,768]{1,0:T(8,128)S(1)}, u32[]{:S(2)}, u32[]{:S(2)}) collective-permute-start(f32[22,768]{1,0:T(8,128)S(1)} %add.405), channel_id=1, source_target_pairs={{0,16},{4,20},{8,24},{12,28},{16,0},{20,4},{24,8},{28,12},{1,17},{... | collective-permute-start | bytes 202760 | tf_op jit(solution)/shard_map/ppermute | solution.py:541
  (63 other events, 306.9 us)
